TPU v7x, 128 devices: a whole 4x4x4 slice. The times are simulated.
128 devices in a mesh: ctx: 16 (over y, z), exp: 8 (over x, core).
Axes of the slice: x: 4, y: 4, z: 4, core: 2. Of those that a mesh axis runs over, the one named last changes fastest.
Arguments:
- query_rows: bfloat16 [2048, 8192], P('ctx', 'exp'), may hold values from -6 to 6
- key_rows: bfloat16 [2048, 8192], P('ctx', 'exp'), may hold values from -6 to 6
- value_rows: bfloat16 [2048, 8192], P('ctx', 'exp'), may hold values from -6 to 6
- log_decay: float32 [64, 2048], P('exp', 'ctx'), may hold values from -2.2 to 0, as said below
- residual: bfloat16 [2048, 6144], P('ctx', 'exp'), may hold values from -6 to 6
- out_weight: bfloat16 [8192, 6144], P('exp', 'ctx'), may hold values from -0.0625 to 0.0625
- router_weight: bfloat16 [6144, 8], replicated, may hold values from -0.0390625 to 0.0390625
- expert_ids: int32 [2048, 2], P('ctx'), may hold values from 0 to 7, all different within a row; in each aligned block of 128 rows (0 to 127, 128 to 255, ...) at most 36 rows name the same one
- expert_gate: bfloat16 [8, 6144, 9216], P('exp', None, 'ctx'), may hold values from -0.078125 to 0.078125
- expert_up: bfloat16 [8, 6144, 9216], P('exp', None, 'ctx'), may hold values from -0.078125 to 0.078125
- expert_down: bfloat16 [8, 9216, 6144], P('exp', 'ctx'), may hold values from -0.0625 to 0.0625
Outputs:
- hidden: bfloat16 [2048, 6144], P('ctx', 'exp')
- mixture: bfloat16 [2048, 6144], P('ctx', 'exp')
Inputs may be any that keep to these rules, and one draw needn't show every extreme that they name: `expert_ids`: the two ids of a row differ. In each aligned block of 128 rows (the rows of one device along ctx) no expert is named by more than 36 rows, and in some block an expert is named by exactly 36 rows. `log_decay`: every entry is negative.
All inputs are finite; a program needn't handle non-finite values.
Results may differ from a plain program's by a relative error of at most 0.035.
Values may be sent and summed in bfloat16 or wider, within the bound.
A program may use at most 128 MiB of HBM per device.

v0:
```python
import jax
import jax.numpy as jnp
from jax import lax
from jax.sharding import PartitionSpec as P

epsilon = 1e-05
highest = lax.Precision.HIGHEST


def carried_in(array, axis, combine, identity):
    size, index = (lax.axis_size(axis), lax.axis_index(axis))
    everything = jax.tree.map(
        lambda part, kind: lax.all_gather(part.astype(kind), axis),
        array,
        (jnp.bfloat16, jnp.bfloat16),
    )
    start = jax.tree.map(
        lambda part, zero: jnp.broadcast_to(jnp.asarray(zero, part.dtype), part.shape),
        array,
        identity,
    )

    def step(k, before):
        reached = k < index
        new = combine(
            before, jax.tree.map(lambda part, own: part[k].astype(own.dtype), everything, array)
        )
        return jax.tree.map(lambda a, b: jnp.where(reached, a, b), new, before)

    return lax.fori_loop(0, size, step, start)


def per_device(
    query_rows,
    key_rows,
    value_rows,
    log_decay,
    residual,
    out_weight,
    router_weight,
    expert_ids,
    expert_gate,
    expert_up,
    expert_down,
):
    length = query_rows.shape[0]
    head_count = log_decay.shape[0]
    head_width = query_rows.shape[1] // head_count
    query_heads = query_rows.reshape(length, head_count, head_width)
    key_heads = key_rows.reshape(length, head_count, head_width)
    value_heads = value_rows.reshape(length, head_count, head_width)
    cumulative = jnp.cumsum(log_decay, axis=1)
    row_index = lax.broadcasted_iota(jnp.int32, (length, length), 0)
    col_index = lax.broadcasted_iota(jnp.int32, (length, length), 1)
    gaps = cumulative[:, :, None] - cumulative[:, None, :]
    mask_weights = jnp.where((col_index <= row_index)[None], jnp.exp(jnp.minimum(gaps, 0.0)), 0.0)
    scores = jnp.einsum("thd,shd->hts", query_heads, key_heads, preferred_element_type=jnp.float32)
    scaled_scores = (scores * mask_weights).astype(jnp.bfloat16)
    inside = jnp.einsum(
        "hts,shd->thd", scaled_scores, value_heads, preferred_element_type=jnp.float32
    )
    block_total = cumulative[:, -1]
    keep_factor = jnp.exp(block_total[:, None] - cumulative)
    weighted_keys = key_heads.astype(jnp.float32) * keep_factor.T[:, :, None]
    block_state = jnp.einsum(
        "thd,the->hde", weighted_keys, value_heads.astype(jnp.float32), precision=highest
    )

    def combine_pair(earlier_pair, later_pair):
        merged_total = earlier_pair[0] + later_pair[0]
        merged_state = jnp.exp(later_pair[0])[:, None, None] * earlier_pair[1] + later_pair[1]
        return (merged_total, merged_state)

    empty_pair = (jnp.zeros_like(block_total), jnp.zeros_like(block_state))
    prior_total, prior_state = carried_in(
        (block_total, block_state), "ctx", combine_pair, empty_pair
    )
    outside = jnp.einsum(
        "thd,hde->the", query_heads.astype(jnp.float32), prior_state, precision=highest
    )
    outside = outside * jnp.exp(cumulative).T[:, :, None]
    attended = inside + outside
    normed = attended * lax.rsqrt(jnp.mean(attended * attended, axis=2, keepdims=True) + epsilon)
    normed = normed.astype(jnp.bfloat16).reshape(length, head_count * head_width)
    partial_value = jnp.dot(
        normed,
        lax.all_gather(out_weight, "ctx", axis=1, tiled=True),
        preferred_element_type=jnp.float32,
    )
    projected = lax.psum_scatter(
        partial_value.astype(jnp.bfloat16), "exp", scatter_dimension=1, tiled=True
    ).astype(jnp.float32)
    hidden = (residual.astype(jnp.float32) + projected).astype(jnp.bfloat16)
    whole = lax.all_gather(hidden, "exp", axis=1, tiled=True)
    wide_rows = whole.astype(jnp.float32)
    scaled = (
        wide_rows * lax.rsqrt(jnp.mean(wide_rows * wide_rows, axis=1, keepdims=True) + epsilon)
    ).astype(jnp.bfloat16)
    logits = jnp.dot(scaled, router_weight, preferred_element_type=jnp.float32)
    expert_count = router_weight.shape[1]
    expert_range = jnp.arange(expert_count, dtype=jnp.int32)
    choice_hot = (expert_ids[:, :, None] == expert_range[None, None, :]).astype(jnp.int32)
    picked = jnp.sum(logits[:, None, :] * choice_hot.astype(jnp.float32), axis=2)
    first_weight = jax.nn.sigmoid(picked[:, 0] - picked[:, 1])
    second_weight = jax.nn.sigmoid(picked[:, 1] - picked[:, 0])
    token_weight = first_weight[:, None] * choice_hot[:, 0, :].astype(jnp.float32) + second_weight[
        :, None
    ] * choice_hot[:, 1, :].astype(jnp.float32)
    counts = jnp.sum(choice_hot, axis=1)
    before = jnp.cumsum(counts, axis=0, dtype=jnp.int32) - counts
    slot_index = jnp.sum(before[:, None, :] * choice_hot, axis=2)
    capacity = 2 * length // lax.axis_size("exp") + length // 32
    slot_hot = (
        slot_index[:, :, None] == jnp.arange(capacity, dtype=jnp.int32)[None, None, :]
    ).astype(jnp.bfloat16)
    dispatch = jnp.einsum(
        "tje,tjc->etc",
        choice_hot.astype(jnp.bfloat16),
        slot_hot,
        preferred_element_type=jnp.float32,
    ).astype(jnp.bfloat16)
    own_expert = lax.axis_index("exp")
    own_dispatch = lax.dynamic_index_in_dim(dispatch, own_expert, 0, keepdims=False)
    slot_input = jnp.einsum(
        "tc,td->cd", own_dispatch, scaled, preferred_element_type=jnp.float32
    ).astype(jnp.bfloat16)
    gate_w = expert_gate[0]
    up_w = expert_up[0]
    down_w = expert_down[0]
    shard_rows = lax.all_gather(slot_input, "ctx", axis=0, tiled=True)
    gate_proj = jnp.dot(shard_rows, gate_w, preferred_element_type=jnp.float32)
    up_proj = jnp.dot(shard_rows, up_w, preferred_element_type=jnp.float32)
    active = (jax.nn.silu(gate_proj) * up_proj).astype(jnp.bfloat16)
    expert_out = lax.psum_scatter(
        jnp.dot(active, down_w, preferred_element_type=jnp.float32).astype(jnp.bfloat16),
        "ctx",
        scatter_dimension=0,
        tiled=True,
    )
    own_weight = lax.dynamic_index_in_dim(token_weight, own_expert, 1, keepdims=False)
    returned = jnp.dot(own_dispatch, expert_out, preferred_element_type=jnp.float32)
    weighted = lax.optimization_barrier((own_weight[:, None] * returned).astype(jnp.bfloat16))
    summed = lax.psum_scatter(
        weighted.astype(jnp.float32).astype(jnp.bfloat16), "exp", scatter_dimension=1, tiled=True
    )
    return (hidden, summed)


def solution(mesh):
    return jax.shard_map(
        per_device,
        mesh=mesh,
        in_specs=(
            P("ctx", "exp"),
            P("ctx", "exp"),
            P("ctx", "exp"),
            P("exp", "ctx"),
            P("ctx", "exp"),
            P("exp", "ctx"),
            P(),
            P("ctx", None),
            P("exp", None, "ctx"),
            P("exp", None, "ctx"),
            P("exp", "ctx", None),
        ),
        out_specs=(P("ctx", "exp"), P("ctx", "exp")),
        check_vma=False,
    )
```

profile of v0, /device:TPU:37, one launch (start us, length us, event | category | flops | bytes accessed | tf_op | source)
XLA Modules:
  0.0 544.6 jit_solution(12196288909111640924)
XLA Ops:
  7.2 1.2 copy.42
  8.4 1.0 reduce_window_sum.22
  9.4 0.2 slice_reduce_fusion
  9.5 0.1 exponential_bitcast_fusion.1
  9.6 1.1 convolution_convert_fusion.3
  10.8 0.7 all-gather.8.cloned.1.call-update
  11.6 1.4 fusion.62
  13.5 0.2 fusion.60
  13.7 0.2 dynamic-update-slice
  13.9 30.4 %all-reduce = bf16[128]{0:T(256)(128)(2,1)S(1)} all-reduce(bf16[128]{0:T(256)(128)(2,1)S(1)} %dynamic-update-slice), channel_id=2, replica_groups=mesh['ctx'=16,'exp'=8] {'ctx'}, use_global_device_ids=true, to_apply=%add | all-reduce | flops 128 | bytes 512
  44.3 0.1 reshape.87
  44.4 20.0 %all-gather.12.cloned.1.call-done = bf16[128,128,128]{2,1,0:T(8,128)(2,1)} async-done(((bf16[8,128,128]{2,1,0:T(8,128)(2,1)}), bf16[128,128,128]{2,1,0:T(8,128)(2,1)}) %all-gather.12.cloned.1.call-update) | async-done | bytes 4194320 | tf_op jit(solution)/shard_map/all_gather | solution.py:13
  64.4 18.3 %while.14 = (s32[]{:T(128)}, f32[8,128,128]{2,1,0:T(8,128)S(1)}, s32[]{:T(128)}, bf16[16,8]{1,0:T(8,128)(2,1)S(1)}, bf16[16,8,128,128]{3,2,1,0:T(8,128)(2,1)}, /*index=5*/s32[]{:T(128)}, s32[]{:T(128)}) while((s32[]{:T(128)}, f32[8,128,128]{2,1,0:T(8,128)S(1)}, s32[]{:T(128)}, bf16[16,8]{1,0:T(8,128)(2,1)S(1)}, ...), condition=%wide.region_2.3_spmd.clone, body=%wide.region_1.2_spmd.clone.sunk | while | flops 655372 | bytes 1310913 | solution.py:30
  64.4 1.1 fusion.79
  65.6 1.1 fusion.79
  66.8 1.1 fusion.79
  67.9 1.1 fusion.79
  69.0 1.1 fusion.79
  70.2 1.1 fusion.79
  71.3 1.1 fusion.79
  72.5 1.1 fusion.79
  73.6 1.1 fusion.79
  74.7 1.1 fusion.79
  75.9 1.1 fusion.79
  77.0 1.1 fusion.79
  78.2 1.1 fusion.79
  79.3 1.1 fusion.79
  80.5 1.1 fusion.79
  81.6 1.1 fusion.79
  82.8 0.6 fusion.18
  83.4 0.5 multiply_reduce_fusion
  83.9 81.0 %all-gather.8.cloned.1.call-done = bf16[1024,6144]{1,0:T(8,128)(2,1)} async-done(((bf16[1024,384]{1,0:T(8,128)(2,1)}), bf16[1024,6144]{1,0:T(8,128)(2,1)}) %all-gather.8.cloned.1.call-update) | async-done | bytes 12582928 | tf_op jit(solution)/shard_map/all_gather | solution.py:87
  164.9 7.7 %convolution_convert_fusion.1 = bf16[128,6144]{1,0:T(8,128)(2,1)} fusion(bf16[128,1024]{0,1:T(8,128)(2,1)S(1)} %bitcast.105, bf16[1024,6144]{1,0:T(8,128)(2,1)} %all-gather.8.cloned.1.call-done), kind=kOutput, calls=%fused_computation.5 | convolution fusion | flops 1611399168 | bytes 14417920 | tf_op jit(solution)/shard_map/dot_general | solution.py:85
  172.6 0.0 all-gather.10.cloned.1.call-start
  172.7 29.4 %reduce-scatter.5.cloned.1.call-done = bf16[128,768]{1,0:T(8,128)(2,1)} async-done(((bf16[128,6144]{1,0:T(8,128)(2,1)}), bf16[128,768]{1,0:T(8,128)(2,1)}) %reduce-scatter.5.cloned.1.call-update) | async-done | bytes 196624 | tf_op jit(solution)/shard_map/reduce_scatter | solution.py:90
  202.0 1.6 add_convert_fusion
  203.8 0.1 copy.39
  203.9 0.1 copy.35
  204.0 0.2 reduce_window_sum.23
  204.3 0.1 copy.38
  204.4 0.5 fusion.39
  204.9 0.1 dynamic-slice_convert_fusion
  204.9 0.1 copy.40
  205.0 25.6 %all-gather.10.cloned.1.call-done = bf16[128,6144]{1,0:T(8,128)(2,1)} async-done(((bf16[128,768]{1,0:T(8,128)(2,1)}), bf16[128,6144]{1,0:T(8,128)(2,1)}) %all-gather.10.cloned.1.call-update) | async-done | bytes 1572880 | tf_op jit(solution)/shard_map/all_gather | solution.py:94
  230.7 1.9 fusion.9
  232.6 2.7 fusion.8
  235.3 0.2 reduce-scatter.7.cloned.1.call-start
  236.2 0.6 fusion.21
  236.8 68.0 %all-gather.14.cloned.1.call-done = bf16[16,36,6144]{2,1,0:T(8,128)(2,1)} async-done(((bf16[1,36,6144]{2,1,0:T(8,128)(2,1)}), bf16[16,36,6144]{2,1,0:T(8,128)(2,1)}) %all-gather.14.cloned.1.call-update) | async-done | bytes 7077904 | tf_op jit(solution)/shard_map/all_gather | solution.py:130
  304.9 8.9 %reshape.93 = bf16[576,6144]{1,0:T(8,128)(2,1)} reshape(bf16[16,36,6144]{2,1,0:T(8,128)(2,1)} %all-gather.14.cloned.1.call-done) | data formatting | bytes 14155776
  313.7 10.1 %fusion.6 = f32[576,576]{1,0:T(8,128)S(1)} fusion(bf16[576,6144]{1,0:T(8,128)(2,1)} %reshape.93, bf16[1,6144,576]{1,2,0:T(8,128)(2,1)} %param.21), kind=kOutput, calls=%fused_computation.10 | convolution fusion | flops 4076863488 | bytes 15482880 | tf_op jit(solution)/shard_map/dot_general | solution.py:131
  323.9 8.9 %fusion.14 = bf16[576,576]{1,0:T(8,128)(2,1)S(1)} fusion(bf16[576,6144]{1,0:T(8,128)(2,1)S(1)} %copy-done.2, bf16[1,6144,576]{1,2,0:T(8,128)(2,1)} %param.22, f32[576,576]{1,0:T(8,128)S(1)} %fusion.6), kind=kOutput, calls=%fused_computation.19 | convolution fusion | flops 4078854144 | bytes 16146432 | tf_op jit(solution)/shard_map/dot_general | solution.py:132
  332.8 7.8 %convolution_convert_fusion = bf16[576,6144]{1,0:T(8,128)(2,1)} fusion(bf16[576,576]{1,0:T(8,128)(2,1)S(1)} %fusion.14, bf16[1,576,6144]{2,1,0:T(8,128)(2,1)S(1)} %bitcast.110), kind=kOutput, calls=%fused_computation.3 | convolution fusion | flops 4080402432 | bytes 14819328 | tf_op jit(solution)/shard_map/dot_general | solution.py:135
  340.5 92.0 %fusion = bf16[48,6144]{1,0:T(8,128)(2,1)S(1)} fusion(bf16[576,6144]{1,0:T(8,128)(2,1)} %convolution_convert_fusion), kind=kCustom, calls=%all-reduce-scatter | all-reduce-scatter fusion | flops 4718593 | bytes 7668224
  432.5 2.9 collective-permute-start.2
  435.4 2.6 collective-permute-start.1
  438.0 4.6 collective-permute-start
  442.7 0.1 slice.24
  442.8 1.4 collective-permute-start.3
  444.2 11.5 %collective-permute-done.3 = bf16[36,6144]{1,0:T(8,128)(2,1)S(1)} collective-permute-done((bf16[36,6144]{1,0:T(8,128)(2,1)S(1)}, bf16[36,6144]{1,0:T(8,128)(2,1)S(1)}, u32[]{:S(2)}, u32[]{:S(2)}) %collective-permute-start.3) | collective-permute-done | bytes 442400
  455.7 9.9 %collective-permute-done = bf16[48,6144]{1,0:T(8,128)(2,1)S(1)} collective-permute-done((bf16[48,6144]{1,0:T(8,128)(2,1)S(1)}, bf16[48,6144]{1,0:T(8,128)(2,1)S(1)}, u32[]{:S(2)}, u32[]{:S(2)}) %collective-permute-start) | collective-permute-done | bytes 589856
  465.6 20.0 %concatenate = bf16[228,6144]{1,0:T(8,128)(2,1)} concatenate(bf16[36,6144]{1,0:T(8,128)(2,1)S(1)} %collective-permute-done.3, bf16[48,6144]{1,0:T(8,128)(2,1)S(1)} %collective-permute-done.2, bf16[48,6144]{1,0:T(8,128)(2,1)S(1)} %collective-permute-done.1, bf16[48,6144]{1,0:T(8,128)(2,1)S(1)} %collective-permute-done, bf16[48,6144]{1,0:T(8,128)(2,1)S(1)} %fusion), dimensions={0} | concatenate | bytes 5603328
  485.6 2.8 fusion.2
  488.5 49.3 %reduce-scatter.7.cloned.1.call-done = bf16[128,768]{1,0:T(8,128)(2,1)} async-done(((bf16[128,6144]{1,0:T(8,128)(2,1)}), bf16[128,768]{1,0:T(8,128)(2,1)}) %reduce-scatter.7.cloned.1.call-update) | async-done | bytes 196624 | tf_op jit(solution)/shard_map/reduce_scatter | solution.py:143
  (63 shorter events, 0.7 us)
Async XLA Ops:
  7.2 2.5 copy-start
  7.2 57.2 %all-gather.12.cloned.1.call-start = ((), (), s32[]{:S(2)}) async-start(), calls=%async_computation.6 | async-start | bytes 4456448 | tf_op jit(solution)/shard_map/all_gather | solution.py:13
  10.8 154.2 %all-gather.8.cloned.1.call-start = ((), (), s32[]{:S(2)}) async-start(), calls=%async_computation.2 | async-start | bytes 13369344 | tf_op jit(solution)/shard_map/all_gather | solution.py:87
  11.5 190.5 %reduce-scatter.5.cloned.1.call-start = ((), (), s32[]{:S(2)}) async-start(), calls=%async_computation.3 | async-start | bytes 1769472 | tf_op jit(solution)/shard_map/reduce_scatter | solution.py:90
  64.4 18.3 %copy-start.4 = (bf16[128,1024]{1,0:T(8,128)(2,1)S(1)}, bf16[128,1024]{1,0:T(8,128)(2,1)}, u32[]{:S(2)}) copy-start(bf16[128,1024]{1,0:T(8,128)(2,1)} %param.13) | copy-start | bytes 786436
  164.9 37.1 %copy-start.5 = (bf16[128,768]{1,0:T(8,128)(2,1)S(1)}, bf16[128,768]{1,0:T(8,128)(2,1)}, u32[]{:S(2)}) copy-start(bf16[128,768]{1,0:T(8,128)(2,1)} %param.17) | copy-start | bytes 589828
  164.9 38.8 %copy-start.6 = (s32[128,2]{0,1:T(2,128)S(1)}, s32[128,2]{0,1:T(2,128)}, u32[]{:S(2)}) copy-start(s32[128,2]{0,1:T(2,128)} %param.20) | copy-start | bytes 3076
  172.6 58.1 %all-gather.10.cloned.1.call-start = ((), (), s32[]{:S(2)}) async-start(), calls=%async_computation.4 | async-start | bytes 1769472 | tf_op jit(solution)/shard_map/all_gather | solution.py:94
  203.7 32.6 %copy-start.7 = (bf16[6144,8]{0,1:T(8,128)(2,1)S(1)}, bf16[6144,8]{0,1:T(8,128)(2,1)}, u32[]{:S(2)}) copy-start(bf16[6144,8]{0,1:T(8,128)(2,1)} %param.19) | copy-start | bytes 294916
  203.7 101.1 %all-gather.14.cloned.1.call-start = ((), (), s32[]{:S(2)}) async-start(), calls=%async_computation.7 | async-start | bytes 8355840 | tf_op jit(solution)/shard_map/all_gather | solution.py:130
  230.7 5.6 %copy-start.3 = (bf16[128,6144]{1,0:T(8,128)(2,1)S(1)}, bf16[128,6144]{1,0:T(8,128)(2,1)}, u32[]{:S(2)}) copy-start(bf16[128,6144]{1,0:T(8,128)(2,1)} %all-gather.10.cloned.1.call-done) | copy-start | bytes 4718596
  235.3 302.4 %reduce-scatter.7.cloned.1.call-start = ((), (), s32[]{:S(2)}) async-start(), calls=%async_computation.5 | async-start | bytes 1769472 | tf_op jit(solution)/shard_map/reduce_scatter | solution.py:143
  313.7 10.1 %copy-start.2 = (bf16[576,6144]{1,0:T(8,128)(2,1)S(1)}, bf16[576,6144]{1,0:T(8,128)(2,1)}, u32[]{:S(2)}) copy-start(bf16[576,6144]{1,0:T(8,128)(2,1)} %reshape.93) | copy-start | bytes 21233668
  313.7 19.0 %slice-start = ((s8[7077888]{0:T(1024)(128)(4,1)}), s8[4194304]{0:T(1024)(128)(4,1)S(1)}, s32[]{:S(2)}) async-start(s8[7077888]{0:T(1024)(128)(4,1)} %bitcast.109), calls=%async_computation.8 | async-start | bytes 8388608
  323.9 8.9 %slice-start.1 = ((s8[7077888]{0:T(1024)(128)(4,1)}), s8[2883584]{0:T(1024)(128)(4,1)S(1)}, s32[]{:S(2)}) async-start(s8[7077888]{0:T(1024)(128)(4,1)} %bitcast.109), calls=%async_computation.9 | async-start | bytes 5767168
  432.5 23.2 %collective-permute-start.2 = (bf16[48,6144]{1,0:T(8,128)(2,1)S(1)}, bf16[48,6144]{1,0:T(8,128)(2,1)S(1)}, u32[]{:S(2)}, u32[]{:S(2)}) collective-permute-start(bf16[48,6144]{1,0:T(8,128)(2,1)S(1)} %fusion), channel_id=1, source_target_pairs={{0,24},{8,32},{16,40},{24,48},{32,56},{40,64},{48,72},{56,80},{64,... | collective-permute-start | bytes 1769480
  435.4 20.3 %collective-permute-start.1 = (bf16[48,6144]{1,0:T(8,128)(2,1)S(1)}, bf16[48,6144]{1,0:T(8,128)(2,1)S(1)}, u32[]{:S(2)}, u32[]{:S(2)}) collective-permute-start(bf16[48,6144]{1,0:T(8,128)(2,1)S(1)} %fusion), channel_id=1, source_target_pairs={{0,16},{8,24},{16,32},{24,40},{32,48},{40,56},{48,64},{56,72},{64,... | collective-permute-start | bytes 1769480
  438.0 27.5 %collective-permute-start = (bf16[48,6144]{1,0:T(8,128)(2,1)S(1)}, bf16[48,6144]{1,0:T(8,128)(2,1)S(1)}, u32[]{:S(2)}, u32[]{:S(2)}) collective-permute-start(bf16[48,6144]{1,0:T(8,128)(2,1)S(1)} %fusion), channel_id=1, source_target_pairs={{0,8},{8,16},{16,24},{24,32},{32,40},{40,48},{48,56},{56,64},{64,7... | collective-permute-start | bytes 1769480
  442.8 12.9 %collective-permute-start.3 = (bf16[36,6144]{1,0:T(8,128)(2,1)S(1)}, bf16[36,6144]{1,0:T(8,128)(2,1)S(1)}, u32[]{:S(2)}, u32[]{:S(2)}) collective-permute-start(bf16[36,6144]{1,0:T(8,128)(2,1)S(1)} %slice.24), channel_id=1, source_target_pairs={{0,32},{8,40},{16,48},{24,56},{32,64},{40,72},{48,80},{56,88},{64,... | collective-permute-start | bytes 1327112
  465.6 72.2 %copy-start.1 = (bf16[128,1024]{1,0:T(8,128)(2,1)S(1)}, bf16[128,1024]{1,0:T(8,128)(2,1)}, u32[]{:S(2)}) copy-start(bf16[128,1024]{1,0:T(8,128)(2,1)} %param.15) | copy-start | bytes 786436
Sparse Core Ops, SparseCore 0:
  10.9 53.4 all-gather.11
  66.5 98.3 all-gather.7
  172.7 29.2 reduce-scatter.4
  204.1 26.4 all-gather.9
  235.4 69.3 all-gather.13
  488.6 49.1 reduce-scatter.6
where the time goes:
time: 552 us; the launch traced here: 545 us
  waiting for transfers between devices  295 us (53%)
  blocking collectives  122 us (22%)
  matrix products  43.2 us (8%)
  local copies, waits for them, and re-layouts  32.9 us (6%)
  other arithmetic  22.7 us (4%)
  between operations  15.6 us (3%)
  starting transfers between devices  11.9 us (2%)
    unnamed x2, blocking collectives  122 us
    all_gather x1, waiting for transfers between devices, per_device(): lax.all_gather(out_weight, 'ctx', axis=1, tiled=True)  81 us
    all_gather x1, waiting for transfers between devices, per_device(): shard_rows = lax.all_gather(slot_input, 'ctx', axis=0, tiled=True)  68 us
    reduce_scatter x1, waiting for transfers between devices, per_device(): lax.psum_scatter(weighted.astype(jnp.float32).astype(jnp.bfloat16), 'exp'...  49.3 us
    unnamed x26, local copies, waits for them, and re-layouts  30.7 us
    reduce_scatter x1, waiting for transfers between devices, per_device(): lax.psum_scatter(partial_value.astype(jnp.bfloat16), 'exp', scatter_dimen...  29.4 us
    all_gather x1, waiting for transfers between devices, per_device(): whole = lax.all_gather(hidden, 'exp', axis=1, tiled=True)  25.6 us
    unnamed x10, waiting for transfers between devices  22.1 us
  transfers between devices with their start and end apart: 10, of which 8 were waited for; matrix products, arithmetic and copies ran while one was open for 4% of the time, Pallas kernels for 0%

commit v1 on v0

--- a/solution.py
+++ b/solution.py
@@ -1,7 +1,251 @@
 import jax
 import jax.numpy as jnp
 from jax import lax
+from jax.experimental import pallas as pl
+from jax.experimental.pallas import tpu as pltpu
+
 from jax.sharding import PartitionSpec as P
+
+MESH = pl.DeviceIdType.MESH
+SIDE = 4
+
+
+def grid_place():
+    me = lax.axis_index("ctx")
+    return me // SIDE, me % SIDE
+
+
+def chunk_at(half, u, v):
+    u, v = (u + SIDE) % SIDE, (v + SIDE) % SIDE
+    return u * SIDE + v if half == 0 else v * SIDE + u
+
+
+def expert_kernel(
+    x_ref, gate_hbm, up_hbm, down_hbm, out_ref,
+    rows, gate_w, up_w, down_w, gate_acc, up_acc, active,
+    rel_out, rel_in, full_out, full_in,
+    weight_sem, g_send, g_recv, r_send, r_recv,
+):
+    y, z = grid_place()
+    half_rows, width = rows.shape[2], rows.shape[3]
+    sub = half_rows // 2
+    place = ((y, z), (z, y))
+    groups = (0, -1, 1, 2)
+    first, second = pl.ds(0, sub), pl.ds(sub, sub)
+
+    def axis_device(half, axis, step):
+        u, v = place[half]
+        return chunk_at(half, u + step, v) if axis == 0 else chunk_at(half, u, v + step)
+
+    weight_copies = [
+        pltpu.make_async_copy(src, dst, weight_sem.at[i])
+        for i, (src, dst) in enumerate(((gate_hbm, gate_w), (up_hbm, up_w), (down_hbm, down_w)))
+    ]
+    for copy in weight_copies:
+        copy.start()
+
+    barrier = pltpu.get_barrier_semaphore()
+    for axis in (0, 1):
+        for step in (1, -1):
+            pl.semaphore_signal(
+                barrier, inc=1, device_id={"ctx": axis_device(0, axis, step)}, device_id_type=MESH
+            )
+    for half in (0, 1):
+        u, v = place[half]
+        rows[half, chunk_at(half, u, v)] = x_ref[pl.ds(half * half_rows, half_rows), :]
+    gate_acc[...] = jnp.zeros_like(gate_acc)
+    up_acc[...] = jnp.zeros_like(up_acc)
+    pl.semaphore_wait(barrier, 4)
+
+    def ring(half, ring_set, kind, step):
+        u, v = place[half]
+        axis = 0 if ring_set == 0 else 1
+        held = (0, 0, -1, 1)[kind] + step
+        if axis == 0:
+            ref = rows.at[half, chunk_at(half, u + held, v)]
+        else:
+            ref = rows.at[half, chunk_at(half, u + groups[ring_set - 1], v + held)]
+        if kind >= 2:
+            ref = ref.at[first if kind == 2 else second]
+        k = (half * 5 + ring_set) * 4 + kind
+        return pltpu.make_async_remote_copy(
+            src_ref=ref, dst_ref=ref, send_sem=g_send.at[k], recv_sem=g_recv.at[k],
+            device_id={"ctx": axis_device(half, axis, 1 if kind % 2 == 0 else -1)}, device_id_type=MESH,
+        )
+
+    def send(half, ring_set, kind):
+        ring(half, ring_set, kind, 0).start()
+
+    def arrive(half, ring_set, kind):
+        ring(half, ring_set, kind, -1 if kind % 2 == 0 else 1).wait_recv()
+
+    def multiply(half, group):
+        u, v = place[half]
+
+        @pl.loop(0, SIDE)
+        def _(i):
+            chunk = chunk_at(half, u + groups[group], i)
+            part = rows[half, chunk]
+            depth = pl.ds(pl.multiple_of(chunk * width, width), width)
+            gate_acc[half] += jnp.dot(part, gate_w[depth, :], preferred_element_type=jnp.float32)
+            up_acc[half] += jnp.dot(part, up_w[depth, :], preferred_element_type=jnp.float32)
+
+    both = (0, 1)
+    for half in both:
+        send(half, 0, 0)
+        send(half, 0, 1)
+    for half in both:
+        send(half, 1, 0)
+        send(half, 1, 1)
+    for half in both:
+        arrive(half, 0, 0)
+        send(half, 0, 2)
+        arrive(half, 0, 1)
+        send(half, 0, 3)
+    for group in (1, 2):
+        for half in both:
+            send(half, group + 1, 0)
+            send(half, group + 1, 1)
+
+    def relay(group):
+        for half in both:
+            arrive(half, group + 1, 0)
+            send(half, group + 1, 2)
+            arrive(half, group + 1, 1)
+            send(half, group + 1, 3)
+
+    def finish(group):
+        for half in both:
+            arrive(half, group + 1, 2)
+            arrive(half, group + 1, 3)
+            multiply(half, group)
+
+    for half in both:
+        arrive(half, 0, 2)
+        arrive(half, 0, 3)
+        send(half, 4, 0)
+        send(half, 4, 1)
+    relay(0)
+    weight_copies[0].wait()
+    weight_copies[1].wait()
+    relay(1)
+    finish(0)
+    relay(2)
+    finish(1)
+    relay(3)
+    finish(2)
+    for half in both:
+        arrive(half, 4, 2)
+        arrive(half, 4, 3)
+        multiply(half, 3)
+        gate = gate_acc[half]
+        active[half] = (gate * (1.0 / (1.0 + jnp.exp(-gate))) * up_acc[half]).astype(active.dtype)
+    weight_copies[2].wait()
+
+    order = (2, 1, -1, 0)
+
+    def product(half, du, dv):
+        u, v = place[half]
+        chunk = chunk_at(half, u + dv, v + du)
+        columns = pl.ds(pl.multiple_of(chunk * width, width), width)
+        return jnp.dot(active[half], down_w[:, columns], preferred_element_type=jnp.float32)
+
+    def reduce_copy(half, group, kind):
+        axis = 1 if group < 4 else 0
+        if kind < 2:
+            part = first if kind == 0 else second
+            src, dst = rel_out.at[half, group, part], rel_in.at[half, group, part]
+        else:
+            src, dst = full_out.at[half, group, kind - 2], full_in.at[half, group, kind - 2]
+        k = (half * 5 + group) * 4 + kind
+        return pltpu.make_async_remote_copy(
+            src_ref=src, dst_ref=dst, send_sem=r_send.at[k], recv_sem=r_recv.at[k],
+            device_id={"ctx": axis_device(half, axis, 1 if kind % 2 == 0 else -1)}, device_id_type=MESH,
+        )
+
+    def far(half, group, value):
+        rel_out[half, group] = value.astype(rel_out.dtype)
+        reduce_copy(half, group, 0).start()
+        reduce_copy(half, group, 1).start()
+
+    def near(half, group, way, value):
+        full_out[half, group, way] = value.astype(full_out.dtype)
+        part = first if way == 0 else second
+        start = way * sub
+        reduce_copy(half, group, way).wait_recv()
+        full_out[half, group, way, part] = (
+            value[start:start + sub] + rel_in[half, group, part].astype(jnp.float32)
+        ).astype(full_out.dtype)
+        reduce_copy(half, group, 2 + way).start()
+
+    def total(half, group, value):
+        for way in (0, 1):
+            reduce_copy(half, group, 2 + way).wait_recv()
+            value = value + full_in[half, group, way].astype(jnp.float32)
+        return value
+
+    for group in range(4):
+        for half in both:
+            far(half, group, product(half, 2, order[group]))
+    for group in range(4):
+        for half in both:
+            near(half, group, 0, product(half, 1, order[group]))
+            near(half, group, 1, product(half, -1, order[group]))
+    for group in range(4):
+        for half in both:
+            value = total(half, group, product(half, 0, order[group]))
+            if group == 0:
+                far(half, 4, value)
+            elif group < 3:
+                near(half, 4, group - 1, value)
+            else:
+                value = total(half, 4, value)
+                out_ref[pl.ds(half * half_rows, half_rows), :] = value.astype(out_ref.dtype)
+
+    for half in both:
+        for ring_set in range(5):
+            for kind in range(4):
+                ring(half, ring_set, kind, 0).wait_send()
+                reduce_copy(half, ring_set, kind).wait_send()
+
+
+def run_experts(x, gate_w, up_w, down_w):
+    slots, width = x.shape
+    half_rows = slots // 2
+    model, units = gate_w.shape
+    blocks = (2, 5, half_rows, width)
+    kind = x.dtype
+    return pl.pallas_call(
+        expert_kernel,
+        out_shape=jax.ShapeDtypeStruct((slots, width), kind),
+        in_specs=[pl.BlockSpec(memory_space=pltpu.VMEM)] + [pl.BlockSpec(memory_space=pl.ANY)] * 3,
+        out_specs=pl.BlockSpec(memory_space=pltpu.VMEM),
+        scratch_shapes=[
+            pltpu.VMEM((2, SIDE * SIDE, half_rows, width), kind),
+            pltpu.VMEM((model, units), kind),
+            pltpu.VMEM((model, units), kind),
+            pltpu.VMEM((units, model), kind),
+            pltpu.VMEM((2, half_rows, units), jnp.float32),
+            pltpu.VMEM((2, half_rows, units), jnp.float32),
+            pltpu.VMEM((2, half_rows, units), kind),
+            pltpu.VMEM(blocks, kind),
+            pltpu.VMEM(blocks, kind),
+            pltpu.VMEM((2, 5, 2, half_rows, width), kind),
+            pltpu.VMEM((2, 5, 2, half_rows, width), kind),
+            pltpu.SemaphoreType.DMA((3,)),
+            pltpu.SemaphoreType.DMA((40,)),
+            pltpu.SemaphoreType.DMA((40,)),
+            pltpu.SemaphoreType.DMA((40,)),
+            pltpu.SemaphoreType.DMA((40,)),
+        ],
+        compiler_params=pltpu.CompilerParams(
+            collective_id=1, has_side_effects=True, vmem_limit_bytes=60 * 1024 * 1024
+        ),
+        cost_estimate=pl.CostEstimate(
+            flops=6 * slots * model * units, bytes_accessed=6 * model * units, transcendentals=0
+        ),
+    )(x, gate_w, up_w, down_w)
+
 
 epsilon = 1e-05
 highest = lax.Precision.HIGHEST
@@ -127,16 +371,9 @@
     gate_w = expert_gate[0]
     up_w = expert_up[0]
     down_w = expert_down[0]
-    shard_rows = lax.all_gather(slot_input, "ctx", axis=0, tiled=True)
-    gate_proj = jnp.dot(shard_rows, gate_w, preferred_element_type=jnp.float32)
-    up_proj = jnp.dot(shard_rows, up_w, preferred_element_type=jnp.float32)
-    active = (jax.nn.silu(gate_proj) * up_proj).astype(jnp.bfloat16)
-    expert_out = lax.psum_scatter(
-        jnp.dot(active, down_w, preferred_element_type=jnp.float32).astype(jnp.bfloat16),
-        "ctx",
-        scatter_dimension=0,
-        tiled=True,
-    )
+    chunk_rows = lax.all_to_all(slot_input, "ctx", split_axis=1, concat_axis=0, tiled=True)
+    chunk_out = run_experts(chunk_rows, gate_w, up_w, down_w)
+    expert_out = lax.all_to_all(chunk_out, "ctx", split_axis=0, concat_axis=1, tiled=True)
     own_weight = lax.dynamic_index_in_dim(token_weight, own_expert, 1, keepdims=False)
     returned = jnp.dot(own_dispatch, expert_out, preferred_element_type=jnp.float32)
     weighted = lax.optimization_barrier((own_weight[:, None] * returned).astype(jnp.bfloat16))

time: 552 us -> 420 us (0.76)
  waiting for transfers between devices: 295 us -> 199 us
  Pallas kernels: 0 us -> 92.1 us
  blocking collectives: 122 us -> 30.4 us
  matrix products: 43.2 us -> 14.6 us
    pallas_call x0 -> x1, Pallas kernels: none -> 92.1 us  [run_experts(): pl.pallas_call(expert_kernel, out_shape=jax.ShapeDtypeStruct((slots, widt...]
    unnamed x2 -> x1, blocking collectives: 122 us -> 30.4 us
    all_gather x1 -> x0, waiting for transfers between devices: 68 us -> none  [per_device(): shard_rows = lax.all_gather(slot_input, 'ctx', axis=0, tiled=True)]
    dot_general x3 -> x0, matrix products: 26.7 us -> none  [the longest x1 10.1 us: per_device(): gate_proj = jnp.dot(shard_rows, gate_w, preferred_element_type=jnp.float32)]
    unnamed x10 -> x5, waiting for transfers between devices: 22.1 us -> 0.76 us
    reduce_scatter x1, waiting for transfers between devices: 49.3 us -> 34.1 us  [per_device(): lax.psum_scatter(weighted.astype(jnp.float32).astype(jnp.bfloat16), 'exp'...]
    all_to_all x0 -> x2, starting transfers between devices: none -> 12.3 us  [the longest x1 6.8 us: per_device(): lax.all_to_all(slot_input, 'ctx', split_axis=1, concat_axis=0, tiled=True)]
    unnamed x4 -> x0, starting transfers between devices: 11.5 us -> none
  transfers between devices with their start and end apart: 10 -> 7, of which waited for: 8 -> 6; matrix products, arithmetic and copies ran while one was open for 4% -> 11% of each run, Pallas kernels for 0% -> 0%
where the time goes in v1:
time: 420 us; the launch traced here: 415 us
  waiting for transfers between devices  199 us (47%)
  Pallas kernels  92.1 us (22%)
  blocking collectives  30.4 us (7%)
  local copies, waits for them, and re-layouts  28.6 us (7%)
  other arithmetic  22.7 us (5%)
  between operations  14.7 us (4%)
  matrix products  14.6 us (3%)
  starting transfers between devices  12.5 us (3%)
    pallas_call x1, Pallas kernels, run_experts(): pl.pallas_call(expert_kernel, out_shape=jax.ShapeDtypeStruct((slots, widt...  92.1 us
    all_gather x1, waiting for transfers between devices, per_device(): lax.all_gather(out_weight, 'ctx', axis=1, tiled=True)  81 us
    reduce_scatter x1, waiting for transfers between devices, per_device(): lax.psum_scatter(weighted.astype(jnp.float32).astype(jnp.bfloat16), 'exp'...  34.1 us
    unnamed x1, blocking collectives  30.4 us
    reduce_scatter x1, waiting for transfers between devices, per_device(): lax.psum_scatter(partial_value.astype(jnp.bfloat16), 'exp', scatter_dimen...  29.4 us
    all_gather x1, waiting for transfers between devices, per_device(): whole = lax.all_gather(hidden, 'exp', axis=1, tiled=True)  25.8 us
    unnamed x22, local copies, waits for them, and re-layouts  22.7 us
    all_gather x1, waiting for transfers between devices, carried_in(): lax.all_gather(part.astype(kind), axis)  20 us
  transfers between devices with their start and end apart: 7, of which 6 were waited for; matrix products, arithmetic and copies ran while one was open for 11% of the time, Pallas kernels for 0%

profile of v1, /device:TPU:37, one launch (start us, length us, event | category | flops | bytes accessed | tf_op | source)
XLA Modules:
  0.0 414.6 jit_solution(5262437545174689943)
XLA Ops:
  7.2 0.0 all-gather.10.cloned.1.call-start
  7.2 1.0 reduce_window_sum.22
  8.2 0.2 slice_reduce_fusion
  8.4 0.1 exponential_bitcast_fusion.1
  8.5 1.1 copy.53
  9.6 1.1 convolution_convert_fusion.2
  10.8 0.0 all-gather.6.cloned.1.call-start
  10.8 0.7 all-gather.6.cloned.1.call-update
  11.5 0.0 reduce-scatter.3.cloned.1.call-start
  11.6 1.3 dynamic-slice.4
  13.5 0.2 fusion.45
  13.7 0.2 dynamic-update-slice
  13.9 30.4 %all-reduce = bf16[128]{0:T(256)(128)(2,1)S(1)} all-reduce(bf16[128]{0:T(256)(128)(2,1)S(1)} %dynamic-update-slice), channel_id=2, replica_groups=mesh['ctx'=16,'exp'=8] {'ctx'}, use_global_device_ids=true, to_apply=%add | all-reduce | flops 128 | bytes 512
  44.3 0.1 reshape.93
  44.4 20.0 %all-gather.10.cloned.1.call-done = bf16[128,128,128]{2,1,0:T(8,128)(2,1)} async-done(((bf16[8,128,128]{2,1,0:T(8,128)(2,1)}), bf16[128,128,128]{2,1,0:T(8,128)(2,1)}) %all-gather.10.cloned.1.call-update) | async-done | bytes 4194320 | tf_op jit(solution)/shard_map/all_gather | solution.py:257
  64.5 18.3 %while.14 = (s32[]{:T(128)}, f32[8,128,128]{2,1,0:T(8,128)S(1)}, s32[]{:T(128)}, bf16[16,8]{1,0:T(8,128)(2,1)S(1)}, bf16[16,8,128,128]{3,2,1,0:T(8,128)(2,1)}, /*index=5*/s32[]{:T(128)}, s32[]{:T(128)}) while((s32[]{:T(128)}, f32[8,128,128]{2,1,0:T(8,128)S(1)}, s32[]{:T(128)}, bf16[16,8]{1,0:T(8,128)(2,1)S(1)}, ...), condition=%wide.region_2.3_spmd.clone, body=%wide.region_1.2_spmd.clone.sunk | while | flops 655372 | bytes 1310913 | solution.py:274
  64.5 1.1 fusion.61
  65.6 1.1 fusion.61
  66.8 1.1 fusion.61
  67.9 1.1 fusion.61
  69.1 1.1 fusion.61
  70.2 1.1 fusion.61
  71.3 1.1 fusion.61
  72.5 1.1 fusion.61
  73.6 1.1 fusion.61
  74.8 1.1 fusion.61
  75.9 1.1 fusion.61
  77.0 1.1 fusion.61
  78.2 1.1 fusion.61
  79.4 1.1 fusion.61
  80.5 1.1 fusion.61
  81.6 1.1 fusion.61
  82.8 0.6 fusion.5
  83.4 0.5 multiply_reduce_fusion
  83.9 81.0 %all-gather.6.cloned.1.call-done = bf16[1024,6144]{1,0:T(8,128)(2,1)} async-done(((bf16[1024,384]{1,0:T(8,128)(2,1)}), bf16[1024,6144]{1,0:T(8,128)(2,1)}) %all-gather.6.cloned.1.call-update) | async-done | bytes 12582928 | tf_op jit(solution)/shard_map/all_gather | solution.py:331
  164.9 7.7 %convolution_convert_fusion = bf16[128,6144]{1,0:T(8,128)(2,1)} fusion(bf16[128,1024]{0,1:T(8,128)(2,1)S(1)} %bitcast.104, bf16[1024,6144]{1,0:T(8,128)(2,1)} %all-gather.6.cloned.1.call-done), kind=kOutput, calls=%fused_computation.4 | convolution fusion | flops 1611399168 | bytes 14417920 | tf_op jit(solution)/shard_map/dot_general | solution.py:329
  172.7 0.0 all-gather.8.cloned.1.call-start
  172.7 29.4 %reduce-scatter.3.cloned.1.call-done = bf16[128,768]{1,0:T(8,128)(2,1)} async-done(((bf16[128,6144]{1,0:T(8,128)(2,1)}), bf16[128,768]{1,0:T(8,128)(2,1)}) %reduce-scatter.3.cloned.1.call-update) | async-done | bytes 196624 | tf_op jit(solution)/shard_map/reduce_scatter | solution.py:334
  202.1 1.6 add_convert_fusion
  203.8 0.1 copy.42
  203.9 0.2 reduce_window_sum.23
  204.1 0.1 copy.45
  204.3 0.1 copy.46
  204.4 0.4 fusion.25
  204.8 0.1 dynamic-slice_convert_fusion
  204.9 0.1 copy.47
  205.0 25.8 %all-gather.8.cloned.1.call-done = bf16[128,6144]{1,0:T(8,128)(2,1)} async-done(((bf16[128,768]{1,0:T(8,128)(2,1)}), bf16[128,6144]{1,0:T(8,128)(2,1)}) %all-gather.8.cloned.1.call-update) | async-done | bytes 1572880 | tf_op jit(solution)/shard_map/all_gather | solution.py:338
  230.8 1.8 fusion.2
  232.6 1.9 convolution_convert_fusion.1
  234.5 0.1 copy.56
  234.7 0.9 copy.48
  235.5 6.8 %all-to-all-start = ((bf16[36,16,384]{2,0,1:T(8,128)(2,1)}), bf16[36,16,384]{2,0,1:T(8,128)(2,1)S(1)}, u32[]{:S(2)}, u32[]{:S(2)}) async-start(bf16[36,16,384]{2,0,1:T(8,128)(2,1)} %copy.48), calls=%async_computation.1 | async-start | bytes 983040 | tf_op jit(solution)/shard_map/all_to_all | solution.py:374
  242.3 10.5 %copy.49 = bf16[1,6144,576]{2,1,0:T(8,128)(2,1)} copy(bf16[1,6144,576]{1,2,0:T(8,128)(2,1)} %param.21) | data formatting | bytes 14155776 | tf_op args[8]
  252.8 10.5 %copy.50 = bf16[1,6144,576]{2,1,0:T(8,128)(2,1)} copy(bf16[1,6144,576]{1,2,0:T(8,128)(2,1)} %param.22) | data formatting | bytes 14155776 | tf_op args[9]
  263.3 0.6 fusion.8
  263.9 0.9 all_to_all.31.x_ref
  264.8 92.1 %shard_map.122 = bf16[576,384]{1,0:T(8,128)(2,1)} custom-call(bf16[576,384]{1,0:T(8,128)(2,1)} %all_to_all.31.x_ref, bf16[6144,576]{1,0:T(8,128)(2,1)} %bitcast.96, bf16[6144,576]{1,0:T(8,128)(2,1)} %bitcast.97, bf16[576,6144]{1,0:T(8,128)(2,1)} %bitcast.108), custom_call_target="tpu_custom_call" | custom-call | flops 12230590464 | bytes 21233664 | tf_op jit(solution)/shard_map/pallas_call | solution.py:218
  356.9 1.9 all_to_all.32
  358.8 5.5 %all-to-all-start.1 = ((bf16[16,36,384]{2,1,0:T(8,128)(2,1)}), bf16[16,36,384]{2,1,0:T(8,128)(2,1)S(1)}, u32[]{:S(2)}, u32[]{:S(2)}) async-start(bf16[16,36,384]{2,1,0:T(8,128)(2,1)} %all_to_all.32), calls=%async_computation.2 | async-start | bytes 983040 | tf_op jit(solution)/shard_map/all_to_all | solution.py:376
  364.4 7.6 %all-to-all-done.1 = bf16[16,36,384]{2,1,0:T(8,128)(2,1)S(1)} async-done(((bf16[16,36,384]{2,1,0:T(8,128)(2,1)}), bf16[16,36,384]{2,1,0:T(8,128)(2,1)S(1)}, u32[]{:S(2)}, u32[]{:S(2)}) %all-to-all-start.1) | async-done | bytes 442400 | tf_op jit(solution)/shard_map/all_to_all | solution.py:376
  372.0 0.1 copy.51
  372.1 0.1 copy.57
  372.2 1.8 fusion.1
  374.0 34.1 %reduce-scatter.5.cloned.1.call-done = bf16[128,768]{1,0:T(8,128)(2,1)} async-done(((bf16[128,6144]{1,0:T(8,128)(2,1)}), bf16[128,768]{1,0:T(8,128)(2,1)}) %reduce-scatter.5.cloned.1.call-update) | async-done | bytes 196624 | tf_op jit(solution)/shard_map/reduce_scatter | solution.py:380
  (53 shorter events, 0.7 us)
Async XLA Ops:
  7.2 2.5 copy-start
  7.2 57.3 %all-gather.10.cloned.1.call-start = ((), (), s32[]{:S(2)}) async-start(), calls=%async_computation.8 | async-start | bytes 4456448 | tf_op jit(solution)/shard_map/all_gather | solution.py:257
  10.8 154.2 %all-gather.6.cloned.1.call-start = ((), (), s32[]{:S(2)}) async-start(), calls=%async_computation.4 | async-start | bytes 13369344 | tf_op jit(solution)/shard_map/all_gather | solution.py:331
  11.5 190.6 %reduce-scatter.3.cloned.1.call-start = ((), (), s32[]{:S(2)}) async-start(), calls=%async_computation.5 | async-start | bytes 1769472 | tf_op jit(solution)/shard_map/reduce_scatter | solution.py:334
  64.5 18.3 %copy-start.3 = (bf16[128,1024]{1,0:T(8,128)(2,1)S(1)}, bf16[128,1024]{1,0:T(8,128)(2,1)}, u32[]{:S(2)}) copy-start(bf16[128,1024]{1,0:T(8,128)(2,1)} %param.13) | copy-start | bytes 786436
  164.9 37.1 %copy-start.4 = (bf16[128,768]{1,0:T(8,128)(2,1)S(1)}, bf16[128,768]{1,0:T(8,128)(2,1)}, u32[]{:S(2)}) copy-start(bf16[128,768]{1,0:T(8,128)(2,1)} %param.17) | copy-start | bytes 589828
  164.9 38.8 %copy-start.5 = (s32[128,2]{0,1:T(2,128)S(1)}, s32[128,2]{0,1:T(2,128)}, u32[]{:S(2)}) copy-start(s32[128,2]{0,1:T(2,128)} %param.20) | copy-start | bytes 3076
  172.7 58.2 %all-gather.8.cloned.1.call-start = ((), (), s32[]{:S(2)}) async-start(), calls=%async_computation.6 | async-start | bytes 1769472 | tf_op jit(solution)/shard_map/all_gather | solution.py:338
  235.5 28.4 %all-to-all-start = ((bf16[36,16,384]{2,0,1:T(8,128)(2,1)}), bf16[36,16,384]{2,0,1:T(8,128)(2,1)S(1)}, u32[]{:S(2)}, u32[]{:S(2)}) async-start(bf16[36,16,384]{2,0,1:T(8,128)(2,1)} %copy.48), calls=%async_computation.1 | async-start | bytes 983040 | tf_op jit(solution)/shard_map/all_to_all | solution.py:374
  252.8 10.5 %copy-start.2 = (bf16[128,6144]{1,0:T(8,128)(2,1)S(1)}, bf16[128,6144]{1,0:T(8,128)(2,1)}, u32[]{:S(2)}) copy-start(bf16[128,6144]{1,0:T(8,128)(2,1)} %all-gather.8.cloned.1.call-done) | copy-start | bytes 4718596
  252.8 10.5 %copy-start.6 = (bf16[6144,8]{0,1:T(8,128)(2,1)S(1)}, bf16[6144,8]{0,1:T(8,128)(2,1)}, u32[]{:S(2)}) copy-start(bf16[6144,8]{0,1:T(8,128)(2,1)} %param.19) | copy-start | bytes 294916
  358.8 13.2 %all-to-all-start.1 = ((bf16[16,36,384]{2,1,0:T(8,128)(2,1)}), bf16[16,36,384]{2,1,0:T(8,128)(2,1)S(1)}, u32[]{:S(2)}, u32[]{:S(2)}) async-start(bf16[16,36,384]{2,1,0:T(8,128)(2,1)} %all_to_all.32), calls=%async_computation.2 | async-start | bytes 983040 | tf_op jit(solution)/shard_map/all_to_all | solution.py:376
  364.3 43.8 %reduce-scatter.5.cloned.1.call-start = ((), (), s32[]{:S(2)}) async-start(), calls=%async_computation.7 | async-start | bytes 1769472 | tf_op jit(solution)/shard_map/reduce_scatter | solution.py:380
  372.0 36.1 %copy-start.1 = (bf16[128,1024]{1,0:T(8,128)(2,1)S(1)}, bf16[128,1024]{1,0:T(8,128)(2,1)}, u32[]{:S(2)}) copy-start(bf16[128,1024]{1,0:T(8,128)(2,1)} %param.15) | copy-start | bytes 786436
Sparse Core Ops, SparseCore 0:
  10.9 53.5 all-gather.9
  66.6 98.3 all-gather.5
  172.8 29.2 reduce-scatter.2
  204.2 26.5 all-gather.7
  374.1 33.9 reduce-scatter.4

commit v2 on v0

v2 whole, which is shorter than its diff:
```python
import jax
import jax.numpy as jnp
from jax import lax
from jax.experimental import pallas as pl
from jax.experimental.pallas import tpu as pltpu
from jax.sharding import PartitionSpec as P

MESH = pl.DeviceIdType.MESH
SIDE = 4
CTX = 16
EXP = 8
PAD = 80
GROUPS = (0, -1, 1, 2)
FAR_FIRST = (2, 1, -1, 0)
BOTH = (0, 1)
epsilon = 1e-05
highest = lax.Precision.HIGHEST


def dot(a, b):
    return jnp.dot(a, b, preferred_element_type=jnp.float32)


def dot_rows(a, b):
    return lax.dot_general(a, b, (((1,), (1,)), ((), ())), preferred_element_type=jnp.float32)


def chunk_at(half, u, v):
    u, v = (u + SIDE) % SIDE, (v + SIDE) % SIDE
    return u * SIDE + v if half == 0 else v * SIDE + u


def plane_device(half, axis, step):
    me = lax.axis_index("ctx")
    y, z = me // SIDE, me % SIDE
    u, v = (y, z) if half == 0 else (z, y)
    return chunk_at(half, u + step, v) if axis == 0 else chunk_at(half, u, v + step)


class Gather:
    def __init__(self, buf, send_sem, recv_sem):
        self.buf, self.send_sem, self.recv_sem = buf, send_sem, recv_sem
        self.half_rows = buf.shape[1] // 2
        me = lax.axis_index("ctx")
        y, z = me // SIDE, me % SIDE
        self.place = ((y, z), (z, y))

    def copy(self, half, ring, kind, step):
        u, v = self.place[half]
        axis = 0 if ring == 0 else 1
        held = (0, 0, -1, 1)[kind] + step
        if axis == 0:
            chunk = chunk_at(half, u + held, v)
        else:
            chunk = chunk_at(half, u + GROUPS[ring - 1], v + held)
        start, size = half * self.half_rows, self.half_rows
        if kind >= 2:
            size = size // 2
            start = start + (kind - 2) * size
        ref = self.buf.at[chunk, pl.ds(start, size)]
        k = (half * 5 + ring) * 4 + kind
        return pltpu.make_async_remote_copy(
            src_ref=ref,
            dst_ref=ref,
            send_sem=self.send_sem.at[k],
            recv_sem=self.recv_sem.at[k],
            device_id={"ctx": plane_device(half, axis, 1 if kind % 2 == 0 else -1)},
            device_id_type=MESH,
        )

    def send(self, half, ring, kind):
        self.copy(half, ring, kind, 0).start()

    def arrive(self, half, ring, kind):
        self.copy(half, ring, kind, -1 if kind % 2 == 0 else 1).wait_recv()

    def begin(self):
        for half in BOTH:
            self.send(half, 0, 0)
            self.send(half, 0, 1)
        for half in BOTH:
            self.send(half, 1, 0)
            self.send(half, 1, 1)

    def first_axis(self):
        for half in BOTH:
            self.arrive(half, 0, 0)
            self.send(half, 0, 2)
            self.arrive(half, 0, 1)
            self.send(half, 0, 3)
        for ring in (2, 3):
            for half in BOTH:
                self.send(half, ring, 0)
                self.send(half, ring, 1)
        for half in BOTH:
            self.arrive(half, 0, 2)
            self.arrive(half, 0, 3)
            self.send(half, 4, 0)
            self.send(half, 4, 1)

    def relay(self, group):
        for half in BOTH:
            self.arrive(half, group + 1, 0)
            self.send(half, group + 1, 2)
            self.arrive(half, group + 1, 1)
            self.send(half, group + 1, 3)

    def settle(self, half, group):
        self.arrive(half, group + 1, 2)
        self.arrive(half, group + 1, 3)

    def drain(self):
        for half in BOTH:
            for ring in range(5):
                for kind in range(4):
                    self.copy(half, ring, kind, 0).wait_send()


class RingSum:
    def __init__(self, rel_out, rel_in, full_out, full_in, send_sem, recv_sem, base, device):
        self.refs = (rel_out, rel_in, full_out, full_in)
        self.send_sem, self.recv_sem, self.base, self.device = send_sem, recv_sem, base, device
        self.sub = rel_out.shape[0] // 2

    def copy(self, kind):
        rel_out, rel_in, full_out, full_in = self.refs
        if kind < 2:
            part = pl.ds(kind * self.sub, self.sub)
            src, dst = rel_out.at[part], rel_in.at[part]
        else:
            src, dst = full_out.at[kind - 2], full_in.at[kind - 2]
        return pltpu.make_async_remote_copy(
            src_ref=src,
            dst_ref=dst,
            send_sem=self.send_sem.at[self.base + kind],
            recv_sem=self.recv_sem.at[self.base + kind],
            device_id=self.device(1 if kind % 2 == 0 else -1),
            device_id_type=MESH,
        )

    def far(self, value):
        rel_out = self.refs[0]
        rel_out[...] = value.astype(rel_out.dtype)
        self.copy(0).start()
        self.copy(1).start()

    def near(self, way, value):
        _, rel_in, full_out, _ = self.refs
        full_out[way] = value.astype(full_out.dtype)
        start = way * self.sub
        part = pl.ds(start, self.sub)
        self.copy(way).wait_recv()
        full_out[way, part] = (
            value[start : start + self.sub] + rel_in[part].astype(jnp.float32)
        ).astype(full_out.dtype)
        self.copy(2 + way).start()

    def total(self, value):
        full_in = self.refs[3]
        for way in BOTH:
            self.copy(2 + way).wait_recv()
            value = value + full_in[way].astype(jnp.float32)
        return value

    def drain(self):
        for kind in range(4):
            self.copy(kind).wait_send()


def layer_kernel(
    normed_ref, residual_ref, out_w, router_ref, ids_ref, gate_hbm, up_hbm, down_hbm,
    hidden_ref, mixture_ref,
    normed_all, pair_out, pair_in, proj_rel_out, proj_rel_in, proj_full_out, proj_full_in,
    res_out, res_in, ids_out, ids_in, hid_out, hid_in, mix_out, mix_in,
    picks, disp_out, disp_in, stat_out, stat_in, scale_out, scale_in, scale_col, token_weight,
    rows, gate_w, up_w, down_w, gate_acc, up_acc, active,
    rel_out, rel_in, full_out, full_in, ret_out, ret_in,
    weight_sem, n_send, n_recv, g_send, g_recv, r_send, r_recv, p_send, p_recv, q_send, q_recv,
    swap_send, swap_recv, d_send, d_recv, s_send, s_recv, c_send, c_recv, b_send, b_recv,
):
    ctx, exp = lax.axis_index("ctx"), lax.axis_index("exp")
    y, z = ctx // SIDE, ctx % SIDE
    x, core = exp // 2, exp % 2
    length, part_width = res_in.shape[1], res_in.shape[2]
    width = rows.shape[2]
    slots = rows.shape[1]
    pair_slots = slots // EXP
    half_rows = slots // 2
    model = down_w.shape[1]
    f32, kind = jnp.float32, rows.dtype
    place = ((y, z), (z, y))

    weight_copies = [
        pltpu.make_async_copy(src, dst, weight_sem.at[i])
        for i, (src, dst) in enumerate(((gate_hbm, gate_w), (up_hbm, up_w), (down_hbm, down_w)))
    ]
    for copy in weight_copies:
        copy.start()

    def partner(i):
        return {"ctx": 2 * exp + i, "exp": ctx // 2}

    def partner_is_me(i):
        return jnp.logical_and(ctx == 2 * exp + i, exp == ctx // 2)

    slot = ctx % 2
    barrier = pltpu.get_barrier_semaphore()

    @pl.loop(1, CTX)
    def _(k):
        pl.semaphore_signal(barrier, inc=1, device_id={"ctx": (ctx + k) % CTX}, device_id_type=MESH)

    @pl.loop(1, EXP)
    def _(k):
        pl.semaphore_signal(barrier, inc=1, device_id={"exp": (exp + k) % EXP}, device_id_type=MESH)

    for i in BOTH:

        @pl.when(jnp.logical_not(partner_is_me(i)))
        def _():
            pl.semaphore_signal(barrier, inc=1, device_id=partner(i), device_id_type=MESH)

    normed_all[ctx] = normed_ref[...]
    ids_out[0:2, :] = ids_ref[...]
    for i in BOTH:
        res_out[i] = residual_ref[:, i * part_width : (i + 1) * part_width]
    gate_acc[...] = jnp.zeros_like(gate_acc)
    up_acc[...] = jnp.zeros_like(up_acc)
    pl.semaphore_wait(barrier, CTX + EXP - 2 + jnp.where(exp == ctx // 2, 1, 2))

    def swap(index, i, src, dst, mine):
        def copy(arriving):
            k = 2 * index
            return pltpu.make_async_remote_copy(
                src_ref=src,
                dst_ref=dst.at[i] if arriving else dst.at[slot],
                send_sem=swap_send.at[k + i],
                recv_sem=swap_recv.at[k + i] if arriving else swap_recv.at[k + slot],
                device_id=partner(i),
                device_id_type=MESH,
            )

        def start():
            @pl.when(partner_is_me(i))
            def _():
                mine()

            @pl.when(jnp.logical_not(partner_is_me(i)))
            def _():
                copy(False).start()

        def arrive():
            @pl.when(jnp.logical_not(partner_is_me(i)))
            def _():
                copy(True).wait_recv()

        def drain():
            @pl.when(jnp.logical_not(partner_is_me(i)))
            def _():
                copy(False).wait_send()

        return start, arrive, drain

    def keep(src, i, dst):
        def mine():
            dst[i] = src[i]

        return mine

    def keep_ids(i):
        def mine():
            ids_in[i] = ids_out[...]

        return mine

    gather = Gather(normed_all, n_send, n_recv)
    gather.begin()
    swaps_res = [swap(0, i, res_out.at[i], res_in, keep(res_out, i, res_in)) for i in BOTH]
    swaps_ids = [swap(1, i, ids_out, ids_in, keep_ids(i)) for i in BOTH]
    for start, _, _ in swaps_res + swaps_ids:
        start()
    gather.first_axis()
    gather.relay(0)
    gather.relay(1)
    for half in BOTH:
        gather.settle(half, 0)
    gather.relay(2)
    for half in BOTH:
        gather.settle(half, 1)
    gather.relay(3)
    for _, arrive, _ in swaps_ids:
        arrive()

    expert_row = lax.broadcasted_iota(jnp.int32, (EXP, length), 0)
    later = (
        lax.broadcasted_iota(jnp.int32, (length, length), 0)
        < lax.broadcasted_iota(jnp.int32, (length, length), 1)
    ).astype(jnp.bfloat16)
    named = []
    for i in BOTH:
        chosen = [expert_row == ids_in[i, k : k + 1, :] for k in BOTH]
        count = chosen[0].astype(f32) + chosen[1].astype(f32)
        before = dot(count.astype(jnp.bfloat16), later)
        key = jnp.where(count > 0.5, before + float(i * (pair_slots // 2)), -1.0)
        named.append((key, chosen))
    key = jnp.concatenate([named[0][0], named[1][0]], axis=1)
    slot_row = lax.broadcasted_iota(jnp.int32, (128, 2 * length), 0).astype(f32)
    for e in range(EXP):
        picks[e] = jnp.where(slot_row == key[e : e + 1, :], 1.0, 0.0).astype(picks.dtype)

    for group in (2, 3):
        for half in BOTH:
            gather.settle(half, group)

    def project(x_to, core_to):
        blocks = normed_all[pl.ds(2 * (x_to * 2 + core_to), 2)]
        return dot(blocks.reshape(2 * length, blocks.shape[2]), out_w[...])

    def pair_copy(i):
        return pltpu.make_async_remote_copy(
            src_ref=pair_out.at[i],
            dst_ref=pair_in.at[i],
            send_sem=p_send.at[i],
            recv_sem=p_recv.at[i],
            device_id={"exp": x * 2 + 1 - core},
            device_id_type=MESH,
        )

    for i, step in enumerate(FAR_FIRST):
        pair_out[i] = project((x + step + SIDE) % SIDE, 1 - core).astype(kind)
        pair_copy(i).start()
    proj_sum = RingSum(
        proj_rel_out, proj_rel_in, proj_full_out, proj_full_in, q_send, q_recv, 0,
        lambda step: {"exp": ((x + step + SIDE) % SIDE) * 2 + core},
    )
    for i, step in enumerate(FAR_FIRST):
        value = project((x + step + SIDE) % SIDE, core)
        pair_copy(i).wait_recv()
        value = value + pair_in[i].astype(f32)
        if i == 0:
            proj_sum.far(value)
        elif i < 3:
            proj_sum.near(i - 1, value)
        else:
            value = proj_sum.total(value)
    for _, arrive, _ in swaps_res:
        arrive()
    hid = (res_in[...].reshape(2 * length, part_width).astype(f32) + value).astype(kind)
    hid_out[...] = hid.reshape(2, length, part_width)

    def disp_copy(k, src_exp):
        return pltpu.make_async_remote_copy(
            src_ref=disp_out.at[(exp + k) % EXP],
            dst_ref=disp_in.at[src_exp],
            send_sem=d_send.at[k],
            recv_sem=d_recv.at[k],
            device_id={"exp": (exp + k) % EXP},
            device_id_type=MESH,
        )

    @pl.loop(1, EXP)
    def _(k):
        to = (exp + k) % EXP
        disp_out[to] = dot(picks[to, pl.ds(0, PAD), :], hid).astype(kind)
        disp_copy(k, exp).start()

    disp_in[exp] = dot(picks[exp, pl.ds(0, PAD), :], hid).astype(kind)

    swaps_hid = [swap(2, i, hid_out.at[i], hid_in, keep(hid_out, i, hid_in)) for i in BOTH]
    for start, _, _ in swaps_hid:
        start()

    wide = hid.astype(f32)
    columns = pl.ds(pl.multiple_of(ctx * width, width), width)
    stat_out[pl.ds(0, EXP), :] = dot_rows(router_ref[:, columns], hid)
    stat_out[pl.ds(EXP, EXP), :] = lax.dot_general(
        jnp.ones((EXP, width), f32), wide * wide, (((1,), (1,)), ((), ())),
        preferred_element_type=f32, precision=highest,
    )
    stat_in[ctx] = stat_out[...]

    def stat_copy(k, src_ctx):
        return pltpu.make_async_remote_copy(
            src_ref=stat_out,
            dst_ref=stat_in.at[src_ctx],
            send_sem=s_send.at[k],
            recv_sem=s_recv.at[k],
            device_id={"ctx": (ctx + k) % CTX},
            device_id_type=MESH,
        )

    @pl.loop(1, CTX)
    def _(k):
        stat_copy(k, ctx).start()

    @pl.loop(1, EXP)
    def _(k):
        disp_copy(k, (exp + EXP - k) % EXP).wait_recv()

    rows[ctx] = (
        disp_in[...].astype(f32)[:, :pair_slots, :].reshape(slots, width).astype(kind)
    )

    def multiply(half, group):
        u, v = place[half]
        part_rows = pl.ds(half * half_rows, half_rows)

        @pl.loop(0, SIDE)
        def _(i):
            chunk = chunk_at(half, u + GROUPS[group], i)
            part = rows[chunk, part_rows, :]
            depth = pl.ds(pl.multiple_of(chunk * width, width), width)
            gate_acc[half] += dot_rows(part, gate_w[:, depth])
            up_acc[half] += dot_rows(part, up_w[:, depth])

    spread = Gather(rows, g_send, g_recv)
    spread.begin()
    spread.first_axis()
    spread.relay(0)

    @pl.loop(1, CTX)
    def _(k):
        stat_copy(k, (ctx + CTX - k) % CTX).wait_recv()

    stats = stat_in[0]
    for k in range(1, CTX):
        stats = stats + stat_in[k]
    row_scale = lax.rsqrt(stats[EXP:, :] * (1.0 / model) + epsilon)
    logits = stats[:EXP, :] * row_scale
    high = row_scale.astype(jnp.bfloat16).astype(f32)
    middle = (row_scale - high).astype(jnp.bfloat16).astype(f32)
    low = row_scale - high - middle
    which = lax.broadcasted_iota(jnp.int32, row_scale.shape, 0)
    thirds = jnp.where(
        which == 0, high, jnp.where(which == 1, middle, jnp.where(which == 2, low, 0.0))
    ).astype(jnp.bfloat16)

    def scale_copy(k, src_exp):
        return pltpu.make_async_remote_copy(
            src_ref=scale_out.at[(exp + k) % EXP],
            dst_ref=scale_in.at[src_exp],
            send_sem=c_send.at[k],
            recv_sem=c_recv.at[k],
            device_id={"exp": (exp + k) % EXP},
            device_id_type=MESH,
        )

    @pl.loop(1, EXP)
    def _(k):
        to = (exp + k) % EXP
        scale_out[to] = dot_rows(thirds, picks[to])
        scale_copy(k, exp).start()

    scale_in[exp] = dot_rows(thirds, picks[exp])

    picked = []
    for k in BOTH:
        chosen = jnp.concatenate([named[0][1][k], named[1][1][k]], axis=1)
        picked.append(jnp.sum(jnp.where(chosen, logits, 0.0), axis=0, keepdims=True))
    first_weight = 1.0 / (1.0 + jnp.exp(picked[1] - picked[0]))
    second_weight = 1.0 / (1.0 + jnp.exp(picked[0] - picked[1]))
    token_weight[...] = jnp.where(
        which == 0, first_weight, jnp.where(which == 1, second_weight, 0.0)
    ).T

    weight_copies[0].wait()
    weight_copies[1].wait()
    spread.relay(1)
    for half in BOTH:
        spread.settle(half, 0)
        multiply(half, 0)
    spread.relay(2)
    for half in BOTH:
        spread.settle(half, 1)
        multiply(half, 1)
    spread.relay(3)

    @pl.loop(1, EXP)
    def _(k):
        scale_copy(k, (exp + EXP - k) % EXP).wait_recv()

    row_scales = jnp.sum(scale_in[...], axis=1).T
    for e in range(EXP):
        scale_col[pl.ds(e * pair_slots, pair_slots), :] = jnp.broadcast_to(
            row_scales[:pair_slots, e : e + 1], (pair_slots, 128)
        )
    for half in BOTH:
        spread.settle(half, 2)
        multiply(half, 2)
    for half in BOTH:
        spread.settle(half, 3)
        multiply(half, 3)
        scale = scale_col[pl.ds(half * half_rows, half_rows), 0:1]
        gate = gate_acc[half] * scale
        up = up_acc[half] * scale
        active[half] = (gate * (1.0 / (1.0 + jnp.exp(-gate))) * up).astype(kind)
    weight_copies[2].wait()

    def product(half, du, dv):
        u, v = place[half]
        chunk = chunk_at(half, u + dv, v + du)
        return dot(active[half], down_w[:, pl.ds(pl.multiple_of(chunk * width, width), width)])

    def ring_device(half, axis):
        return lambda step: {"ctx": plane_device(half, axis, step)}

    sums = [
        [
            RingSum(
                rel_out.at[half, group], rel_in.at[half, group],
                full_out.at[half, group], full_in.at[half, group],
                r_send, r_recv, (half * 5 + group) * 4, ring_device(half, 1 if group < 4 else 0),
            )
            for group in range(5)
        ]
        for half in BOTH
    ]

    def back_copy(k, src_exp):
        return pltpu.make_async_remote_copy(
            src_ref=ret_out.at[(exp + k) % EXP],
            dst_ref=ret_in.at[src_exp],
            send_sem=b_send.at[k],
            recv_sem=b_recv.at[k],
            device_id={"exp": (exp + k) % EXP},
            device_id_type=MESH,
        )

    for group in range(4):
        for half in BOTH:
            sums[half][group].far(product(half, 2, FAR_FIRST[group]))
    for group in range(4):
        for half in BOTH:
            sums[half][group].near(0, product(half, 1, FAR_FIRST[group]))
            sums[half][group].near(1, product(half, -1, FAR_FIRST[group]))
    blank = jnp.zeros((PAD - pair_slots, width), f32)
    for group in range(4):
        for half in BOTH:
            value = sums[half][group].total(product(half, 0, FAR_FIRST[group]))
            if group == 0:
                sums[half][4].far(value)
            elif group < 3:
                sums[half][4].near(group - 1, value)
            else:
                value = sums[half][4].total(value)
                for i in range(EXP // 2):
                    part = value[i * pair_slots : (i + 1) * pair_slots]
                    ret_out[half * (EXP // 2) + i] = jnp.concatenate([part, blank], axis=0).astype(kind)

    @pl.loop(1, EXP)
    def _(k):
        back_copy(k, exp).start()

    ret_in[exp] = ret_out[exp]

    @pl.loop(1, EXP)
    def _(k):
        back_copy(k, (exp + EXP - k) % EXP).wait_recv()

    back = ret_in[...].reshape(EXP * PAD, width)
    weighted = []
    for k in BOTH:
        chosen = jnp.concatenate([named[0][1][k], named[1][1][k]], axis=1)
        take = jnp.concatenate(
            [
                jnp.where(chosen[e : e + 1, :], picks[e, pl.ds(0, PAD), :].astype(f32), 0.0)
                for e in range(EXP)
            ],
            axis=0,
        ).T.astype(kind)
        weighted.append((dot(take, back) * token_weight[:, k : k + 1]).astype(kind).astype(f32))
    mix_out[...] = (weighted[0] + weighted[1]).astype(kind).reshape(2, length, part_width)
    swaps_mix = [swap(3, i, mix_out.at[i], mix_in, keep(mix_out, i, mix_in)) for i in BOTH]
    for start, _, _ in swaps_mix:
        start()
    for _, arrive, _ in swaps_hid + swaps_mix:
        arrive()
    for i in BOTH:
        hidden_ref[:, i * part_width : (i + 1) * part_width] = hid_in[i]
        mixture_ref[:, i * part_width : (i + 1) * part_width] = mix_in[i]

    gather.drain()
    spread.drain()
    proj_sum.drain()
    for i in range(4):
        pair_copy(i).wait_send()
    for half in BOTH:
        for group in range(5):
            sums[half][group].drain()
    for _, _, drain in swaps_res + swaps_ids + swaps_hid + swaps_mix:
        drain()

    @pl.loop(1, EXP)
    def _(k):
        disp_copy(k, exp).wait_send()
        scale_copy(k, exp).wait_send()
        back_copy(k, exp).wait_send()

    @pl.loop(1, CTX)
    def _(k):
        stat_copy(k, ctx).wait_send()


def project_and_mix(normed, residual, out_weight, router, ids, gate_w, up_w, down_w):
    length, inner = normed.shape
    width = out_weight.shape[1]
    units, model = down_w.shape
    slots = CTX * (2 * length // EXP + length // 32)
    half_rows = slots // 2
    kind, f32 = normed.dtype, jnp.float32
    vmem = pl.BlockSpec(memory_space=pltpu.VMEM)
    anywhere = pl.BlockSpec(memory_space=pl.ANY)
    two = (2, length, width)
    dma = pltpu.SemaphoreType.DMA
    out = jax.ShapeDtypeStruct(residual.shape, kind)
    blocks = (2, 5, half_rows, width)
    return pl.pallas_call(
        layer_kernel,
        out_shape=(out, out),
        in_specs=[vmem] * 5 + [anywhere] * 3,
        out_specs=(vmem, vmem),
        scratch_shapes=[
            pltpu.VMEM((CTX, length, inner), kind),
            pltpu.VMEM((4, 2 * length, width), kind),
            pltpu.VMEM((4, 2 * length, width), kind),
            pltpu.VMEM((2 * length, width), kind),
            pltpu.VMEM((2 * length, width), kind),
            pltpu.VMEM((2, 2 * length, width), kind),
            pltpu.VMEM((2, 2 * length, width), kind),
            pltpu.VMEM(two, kind),
            pltpu.VMEM(two, kind),
            pltpu.VMEM((8, length), jnp.int32),
            pltpu.VMEM((2, 8, length), jnp.int32),
            pltpu.VMEM(two, kind),
            pltpu.VMEM(two, kind),
            pltpu.VMEM(two, kind),
            pltpu.VMEM(two, kind),
            pltpu.VMEM((EXP, 128, 2 * length), kind),
            pltpu.VMEM((EXP, PAD, width), kind),
            pltpu.VMEM((EXP, PAD, width), kind),
            pltpu.VMEM((2 * EXP, 2 * length), f32),
            pltpu.VMEM((CTX, 2 * EXP, 2 * length), f32),
            pltpu.VMEM((EXP, 8, 128), f32),
            pltpu.VMEM((EXP, 8, 128), f32),
            pltpu.VMEM((slots, 128), f32),
            pltpu.VMEM((2 * length, 8), f32),
            pltpu.VMEM((CTX, slots, width), kind),
            pltpu.VMEM((units, model), kind),
            pltpu.VMEM((units, model), kind),
            pltpu.VMEM((units, model), kind),
            pltpu.VMEM((2, half_rows, units), f32),
            pltpu.VMEM((2, half_rows, units), f32),
            pltpu.VMEM((2, half_rows, units), kind),
            pltpu.VMEM(blocks, kind),
            pltpu.VMEM(blocks, kind),
            pltpu.VMEM((2, 5, 2, half_rows, width), kind),
            pltpu.VMEM((2, 5, 2, half_rows, width), kind),
            pltpu.VMEM((EXP, PAD, width), kind),
            pltpu.VMEM((EXP, PAD, width), kind),
            dma((3,)), dma((40,)), dma((40,)), dma((40,)), dma((40,)), dma((40,)), dma((40,)),
            dma((4,)), dma((4,)), dma((4,)), dma((4,)), dma((8,)), dma((8,)),
            dma((EXP,)), dma((EXP,)), dma((CTX,)), dma((CTX,)),
            dma((EXP,)), dma((EXP,)), dma((EXP,)), dma((EXP,)),
        ],
        compiler_params=pltpu.CompilerParams(
            collective_id=1, has_side_effects=True, vmem_limit_bytes=62 * 1024 * 1024
        ),
        cost_estimate=pl.CostEstimate(
            flops=6 * slots * model * units, bytes_accessed=6 * model * units, transcendentals=0
        ),
    )(normed, residual, out_weight, router, ids, gate_w, up_w, down_w)


def carried_in(array, axis, combine, identity):
    size, index = (lax.axis_size(axis), lax.axis_index(axis))
    everything = jax.tree.map(
        lambda part, kind: lax.all_gather(part.astype(kind), axis),
        array,
        (jnp.bfloat16, jnp.bfloat16),
    )
    start = jax.tree.map(
        lambda part, zero: jnp.broadcast_to(jnp.asarray(zero, part.dtype), part.shape),
        array,
        identity,
    )

    def step(k, before):
        reached = k < index
        new = combine(
            before, jax.tree.map(lambda part, own: part[k].astype(own.dtype), everything, array)
        )
        return jax.tree.map(lambda a, b: jnp.where(reached, a, b), new, before)

    return lax.fori_loop(0, size, step, start)


def per_device(
    query_rows,
    key_rows,
    value_rows,
    log_decay,
    residual,
    out_weight,
    router_weight,
    expert_ids,
    expert_gate,
    expert_up,
    expert_down,
):
    length = query_rows.shape[0]
    head_count = log_decay.shape[0]
    head_width = query_rows.shape[1] // head_count
    query_heads = query_rows.reshape(length, head_count, head_width)
    key_heads = key_rows.reshape(length, head_count, head_width)
    value_heads = value_rows.reshape(length, head_count, head_width)
    cumulative = jnp.cumsum(log_decay, axis=1)
    row_index = lax.broadcasted_iota(jnp.int32, (length, length), 0)
    col_index = lax.broadcasted_iota(jnp.int32, (length, length), 1)
    gaps = cumulative[:, :, None] - cumulative[:, None, :]
    mask_weights = jnp.where((col_index <= row_index)[None], jnp.exp(jnp.minimum(gaps, 0.0)), 0.0)
    scores = jnp.einsum("thd,shd->hts", query_heads, key_heads, preferred_element_type=jnp.float32)
    scaled_scores = (scores * mask_weights).astype(jnp.bfloat16)
    inside = jnp.einsum(
        "hts,shd->thd", scaled_scores, value_heads, preferred_element_type=jnp.float32
    )
    block_total = cumulative[:, -1]
    keep_factor = jnp.exp(block_total[:, None] - cumulative)
    weighted_keys = key_heads.astype(jnp.float32) * keep_factor.T[:, :, None]
    block_state = jnp.einsum(
        "thd,the->hde", weighted_keys, value_heads.astype(jnp.float32), precision=highest
    )

    def combine_pair(earlier_pair, later_pair):
        merged_total = earlier_pair[0] + later_pair[0]
        merged_state = jnp.exp(later_pair[0])[:, None, None] * earlier_pair[1] + later_pair[1]
        return (merged_total, merged_state)

    empty_pair = (jnp.zeros_like(block_total), jnp.zeros_like(block_state))
    prior_total, prior_state = carried_in(
        (block_total, block_state), "ctx", combine_pair, empty_pair
    )
    outside = jnp.einsum(
        "thd,hde->the", query_heads.astype(jnp.float32), prior_state, precision=highest
    )
    outside = outside * jnp.exp(cumulative).T[:, :, None]
    attended = inside + outside
    normed = attended * lax.rsqrt(jnp.mean(attended * attended, axis=2, keepdims=True) + epsilon)
    normed = normed.astype(jnp.bfloat16).reshape(length, head_count * head_width)
    return project_and_mix(
        normed,
        residual,
        out_weight,
        router_weight.T,
        expert_ids.T,
        expert_gate[0].T,
        expert_up[0].T,
        expert_down[0],
    )


def solution(mesh):
    return jax.shard_map(
        per_device,
        mesh=mesh,
        in_specs=(
            P("ctx", "exp"),
            P("ctx", "exp"),
            P("ctx", "exp"),
            P("exp", "ctx"),
            P("ctx", "exp"),
            P("exp", "ctx"),
            P(),
            P("ctx", None),
            P("exp", None, "ctx"),
            P("exp", None, "ctx"),
            P("exp", "ctx", None),
        ),
        out_specs=(P("ctx", "exp"), P("ctx", "exp")),
        check_vma=False,
    )
```

time: 552 us -> 277 us (0.50)
  waiting for transfers between devices: 295 us -> 20.8 us
  Pallas kernels: 0 us -> 180 us
  blocking collectives: 122 us -> 30.4 us
  matrix products: 43.2 us -> 2.18 us
  local copies, waits for them, and re-layouts: 32.9 us -> 7.16 us
  starting transfers between devices: 11.9 us -> 0.04 us
    pallas_call x0 -> x1, Pallas kernels: none -> 180 us  [project_and_mix(): pl.pallas_call(layer_kernel, out_shape=(out, out), in_specs=[vmem] * 5 +...]
    all_gather x3 -> x0, waiting for transfers between devices: 175 us -> none  [the longest x1 81 us: per_device(): lax.all_gather(out_weight, 'ctx', axis=1, tiled=True)]
    unnamed x2 -> x1, blocking collectives: 122 us -> 30.4 us
    reduce_scatter x2 -> x0, waiting for transfers between devices: 78.7 us -> none  [the longest x1 49.3 us: per_device(): lax.psum_scatter(weighted.astype(jnp.float32).astype(jnp.bfloat16), 'exp'...]
    dot_general x8 -> x0, matrix products: 41 us -> none  [the longest x1 10.1 us: per_device(): gate_proj = jnp.dot(shard_rows, gate_w, preferred_element_type=jnp.float32)]
    unnamed x26 -> x9, local copies, waits for them, and re-layouts: 30.7 us -> 4.74 us
    unnamed x10 -> x1, waiting for transfers between devices: 22.1 us -> 0.02 us
    unnamed x4 -> x0, starting transfers between devices: 11.5 us -> none
  transfers between devices with their start and end apart: 10 -> 1, of which waited for: 8 -> 1; matrix products, arithmetic and copies ran while one was open for 4% -> 1% of each run, Pallas kernels for 0% -> 0%
where the time goes in v2:
time: 277 us; the launch traced here: 275 us
  Pallas kernels  180 us (65%)
  blocking collectives  30.4 us (11%)
  waiting for transfers between devices  20.8 us (8%)
  other arithmetic  18.8 us (7%)
  between operations  14.8 us (5%)
  local copies, waits for them, and re-layouts  7.16 us (3%)
    pallas_call x1, Pallas kernels, project_and_mix(): pl.pallas_call(layer_kernel, out_shape=(out, out), in_specs=[vmem] * 5 +...  180 us
    unnamed x1, blocking collectives  30.4 us
    all_gather x1, waiting for transfers between devices, carried_in(): lax.all_gather(part.astype(kind), axis)  20.8 us
    select_n x16, other arithmetic, step(): return jax.tree.map(lambda a, b: jnp.where(reached, a, b), new, before)  17.5 us
  transfers between devices with their start and end apart: 1, of which 1 were waited for; matrix products, arithmetic and copies ran while one was open for 1% of the time, Pallas kernels for 0%

profile of v2, /device:TPU:37, one launch (start us, length us, event | category | flops | bytes accessed | tf_op | source)
XLA Modules:
  0.0 274.8 jit_solution(9049598582542992128)
XLA Ops:
  7.2 0.0 copy-start
  7.2 0.0 copy-start.1
  7.2 0.0 all-gather.4.cloned.1.call-start
  7.2 1.0 reduce_window_sum.11
  8.2 0.2 slice_reduce_fusion
  8.4 0.1 exponential_bitcast_fusion.1
  8.5 1.1 copy.35
  9.6 0.0 copy-done
  9.7 1.1 convolution_convert_fusion
  10.7 0.0 all-gather.4.cloned.1.call-update
  10.8 1.2 dynamic-slice
  12.7 0.2 fusion.25
  12.9 0.2 dynamic-update-slice
  13.1 30.4 %all-reduce = bf16[128]{0:T(256)(128)(2,1)S(1)} all-reduce(bf16[128]{0:T(256)(128)(2,1)S(1)} %dynamic-update-slice), channel_id=2, replica_groups=mesh['ctx'=16,'exp'=8] {'ctx'}, use_global_device_ids=true, to_apply=%add | all-reduce | flops 128 | bytes 512
  43.5 0.1 reshape.63
  43.6 20.8 %all-gather.4.cloned.1.call-done = bf16[128,128,128]{2,1,0:T(8,128)(2,1)} async-done(((bf16[8,128,128]{2,1,0:T(8,128)(2,1)}), bf16[128,128,128]{2,1,0:T(8,128)(2,1)}) %all-gather.4.cloned.1.call-update) | async-done | bytes 4194320 | tf_op jit(solution)/shard_map/all_gather | solution.py:677
  64.4 18.1 %while.14 = (s32[]{:T(128)}, f32[8,128,128]{2,1,0:T(8,128)S(1)}, s32[]{:T(128)}, bf16[16,8]{1,0:T(8,128)(2,1)S(1)}, bf16[16,8,128,128]{3,2,1,0:T(8,128)(2,1)}, /*index=5*/s32[]{:T(128)}, s32[]{:T(128)}) while((s32[]{:T(128)}, f32[8,128,128]{2,1,0:T(8,128)S(1)}, s32[]{:T(128)}, bf16[16,8]{1,0:T(8,128)(2,1)S(1)}, ...), condition=%wide.region_2.3_spmd.clone, body=%wide.region_1.2_spmd.clone.sunk | while | flops 655372 | bytes 1310905 | solution.py:694
  64.4 1.1 fusion.36
  65.5 1.1 fusion.36
  66.7 1.1 fusion.36
  67.8 1.1 fusion.36
  68.9 1.1 fusion.36
  70.1 1.1 fusion.36
  71.2 1.1 fusion.36
  72.3 1.1 fusion.36
  73.5 1.1 fusion.36
  74.6 1.1 fusion.36
  75.7 1.1 fusion.36
  76.9 1.1 fusion.36
  78.0 1.1 fusion.36
  79.2 1.1 fusion.36
  80.3 1.1 fusion.36
  81.4 1.1 fusion.36
  82.5 0.0 copy-done.1
  82.5 0.6 fusion.2
  83.1 0.5 multiply_reduce_fusion
  83.7 0.8 copy.34.normed_ref
  84.5 180.2 %shard_map.122 = (bf16[128,768]{1,0:T(8,128)(2,1)}, bf16[128,768]{1,0:T(8,128)(2,1)}) custom-call(bf16[128,1024]{1,0:T(8,128)(2,1)} %copy.34.normed_ref, bf16[128,768]{1,0:T(8,128)(2,1)} %residual_ref.1, bf16[1024,384]{1,0:T(8,128)(2,1)} %out_w.1, bf16[8,6144]{1,0:T(8,128)(2,1)} %bitcast.73, s32[2,128]{1,0:T(2,128)} %bitcast.74, bf16[576,6144]{1,0:T(8,128)(2,1)} %bitcast.70, ...), custom_call_target="tpu_custom_call" | custom-call | flops 12230590464 | bytes 21233664 | tf_op jit(solution)/shard_map/pallas_call | solution.py:617
  264.7 1.6 copy.68
  266.3 1.6 copy.69
  (21 shorter events, 0.3 us)
Async XLA Ops:
  7.2 2.5 copy-start
  7.2 75.3 %copy-start.1 = (bf16[128,1024]{1,0:T(8,128)(2,1)S(1)}, bf16[128,1024]{1,0:T(8,128)(2,1)}, u32[]{:S(2)}) copy-start(bf16[128,1024]{1,0:T(8,128)(2,1)} %param.13) | copy-start | bytes 786436
  7.2 57.2 %all-gather.4.cloned.1.call-start = ((), (), s32[]{:S(2)}) async-start(), calls=%async_computation | async-start | bytes 4456448 | tf_op jit(solution)/shard_map/all_gather | solution.py:677
Sparse Core Ops, SparseCore 0:
  10.9 53.4 all-gather.3

commit v3 on v2

--- a/solution.py
+++ b/solution.py
@@ -168,14 +168,15 @@
 
 
 def layer_kernel(
-    normed_ref, residual_ref, out_w, router_ref, ids_ref, gate_hbm, up_hbm, down_hbm,
+    query_ref, key_ref, value_ref, decay_ref,
+    residual_ref, out_w, router_ref, ids_ref, gate_hbm, up_hbm, down_hbm,
     hidden_ref, mixture_ref,
-    normed_all, pair_out, pair_in, proj_rel_out, proj_rel_in, proj_full_out, proj_full_in,
+    fresh_out, fresh_in, prior_out, prior_in, inside, normed_all, pair_out, pair_in, proj_rel_out, proj_rel_in, proj_full_out, proj_full_in,
     res_out, res_in, ids_out, ids_in, hid_out, hid_in, mix_out, mix_in,
     picks, disp_out, disp_in, stat_out, stat_in, scale_out, scale_in, scale_col, token_weight,
     rows, gate_w, up_w, down_w, gate_acc, up_acc, active,
     rel_out, rel_in, full_out, full_in, ret_out, ret_in,
-    weight_sem, n_send, n_recv, g_send, g_recv, r_send, r_recv, p_send, p_recv, q_send, q_recv,
+    weight_sem, f_send, f_recv, o_send, o_recv, n_send, n_recv, g_send, g_recv, r_send, r_recv, p_send, p_recv, q_send, q_recv,
     swap_send, swap_recv, d_send, d_recv, s_send, s_recv, c_send, c_recv, b_send, b_recv,
 ):
     ctx, exp = lax.axis_index("ctx"), lax.axis_index("exp")
@@ -220,7 +221,35 @@
         def _():
             pl.semaphore_signal(barrier, inc=1, device_id=partner(i), device_id_type=MESH)
 
-    normed_all[ctx] = normed_ref[...]
+    heads = decay_ref.shape[0]
+    head = query_ref.shape[1] // heads
+    row_index = lax.broadcasted_iota(jnp.int32, (length, length), 0)
+    col_index = lax.broadcasted_iota(jnp.int32, (length, length), 1)
+    cum_row = jnp.dot(
+        decay_ref[...], (row_index <= col_index).astype(f32),
+        preferred_element_type=f32, precision=highest,
+    )
+    cum_col = cum_row.T
+    block_total = cum_row[:, length - 1 : length]
+    keep = jnp.exp(block_total - cum_row).T
+    block_keep = jnp.broadcast_to(jnp.exp(block_total), (heads, head))
+    keep_high = block_keep.astype(kind)
+    keep_low = (block_keep - keep_high.astype(f32)).astype(kind)
+    part_rows = head // 2
+    line = lax.broadcasted_iota(jnp.int32, (16, head), 0)
+    for h in range(heads):
+        lanes = slice(h * head, (h + 1) * head)
+        weighted = (key_ref[:, lanes].astype(f32) * keep[:, h : h + 1]).astype(kind)
+        state = lax.dot_general(
+            weighted, value_ref[:, lanes], (((0,), (0,)), ((), ())), preferred_element_type=f32
+        ).astype(kind)
+        factor = jnp.where(
+            line == 0, keep_high[h : h + 1].astype(f32),
+            jnp.where(line == 1, keep_low[h : h + 1].astype(f32), 0.0),
+        ).astype(kind)
+        for i in BOTH:
+            fresh_out[2 * h + i, 0:part_rows] = state[i * part_rows : (i + 1) * part_rows]
+            fresh_out[2 * h + i, part_rows : part_rows + 16] = factor
     ids_out[0:2, :] = ids_ref[...]
     for i in BOTH:
         res_out[i] = residual_ref[:, i * part_width : (i + 1) * part_width]
@@ -261,22 +290,83 @@
 
         return start, arrive, drain
 
-    def keep(src, i, dst):
+    def stay(src, i, dst):
         def mine():
             dst[i] = src[i]
 
         return mine
 
-    def keep_ids(i):
+    def stay_ids(i):
         def mine():
             ids_in[i] = ids_out[...]
 
         return mine
 
+    def state_copy(k, src_ctx):
+        return pltpu.make_async_remote_copy(
+            src_ref=fresh_out.at[(ctx + k) % CTX],
+            dst_ref=fresh_in.at[src_ctx],
+            send_sem=f_send.at[k],
+            recv_sem=f_recv.at[k],
+            device_id={"ctx": (ctx + k) % CTX},
+            device_id_type=MESH,
+        )
+
+    def prior_copy(k, src_ctx):
+        return pltpu.make_async_remote_copy(
+            src_ref=prior_out.at[(ctx + k) % CTX],
+            dst_ref=prior_in.at[src_ctx],
+            send_sem=o_send.at[k],
+            recv_sem=o_recv.at[k],
+            device_id={"ctx": (ctx + k) % CTX},
+            device_id_type=MESH,
+        )
+
+    @pl.loop(1, CTX)
+    def _(k):
+        state_copy(k, ctx).start()
+
+    fresh_in[ctx] = fresh_out[ctx]
+    for h in range(heads):
+        lanes = slice(h * head, (h + 1) * head)
+        scores = dot_rows(query_ref[:, lanes], key_ref[:, lanes])
+        gaps = cum_col[:, h : h + 1] - cum_row[h : h + 1, :]
+        decayed = jnp.where(col_index <= row_index, jnp.exp(jnp.minimum(gaps, 0.0)), 0.0)
+        inside[:, lanes] = dot((scores * decayed).astype(kind), value_ref[:, lanes])
+
+    @pl.loop(1, CTX)
+    def _(k):
+        state_copy(k, (ctx + CTX - k) % CTX).wait_recv()
+
+    state = jnp.zeros((part_rows, head), f32)
+    for j in range(CTX):
+        prior_out[j] = state.astype(kind)
+        if j < CTX - 1:
+            factor = fresh_in[j, part_rows : part_rows + 16].astype(f32)
+            state = (factor[0:1] + factor[1:2]) * state + fresh_in[j, 0:part_rows].astype(f32)
+
+    @pl.loop(1, CTX)
+    def _(k):
+        prior_copy(k, ctx).start()
+
+    prior_in[ctx] = prior_out[ctx]
+    grown = jnp.exp(cum_col)
+
+    @pl.loop(1, CTX)
+    def _(k):
+        prior_copy(k, (ctx + CTX - k) % CTX).wait_recv()
+
+    for h in range(heads):
+        lanes = slice(h * head, (h + 1) * head)
+        before_block = prior_in[2 * h : 2 * h + 2].reshape(head, head)
+        attended = inside[:, lanes] + dot(query_ref[:, lanes], before_block) * grown[:, h : h + 1]
+        square = jnp.mean(attended * attended, axis=1, keepdims=True)
+        normed_all[ctx, :, lanes] = (attended * lax.rsqrt(square + epsilon)).astype(kind)
+
     gather = Gather(normed_all, n_send, n_recv)
     gather.begin()
-    swaps_res = [swap(0, i, res_out.at[i], res_in, keep(res_out, i, res_in)) for i in BOTH]
-    swaps_ids = [swap(1, i, ids_out, ids_in, keep_ids(i)) for i in BOTH]
+    swaps_res = [swap(0, i, res_out.at[i], res_in, stay(res_out, i, res_in)) for i in BOTH]
+    swaps_ids = [swap(1, i, ids_out, ids_in, stay_ids(i)) for i in BOTH]
     for start, _, _ in swaps_res + swaps_ids:
         start()
     gather.first_axis()
@@ -366,7 +456,7 @@
 
     disp_in[exp] = dot(picks[exp, pl.ds(0, PAD), :], hid).astype(kind)
 
-    swaps_hid = [swap(2, i, hid_out.at[i], hid_in, keep(hid_out, i, hid_in)) for i in BOTH]
+    swaps_hid = [swap(2, i, hid_out.at[i], hid_in, stay(hid_out, i, hid_in)) for i in BOTH]
     for start, _, _ in swaps_hid:
         start()
 
@@ -570,7 +660,7 @@
         ).T.astype(kind)
         weighted.append((dot(take, back) * token_weight[:, k : k + 1]).astype(kind).astype(f32))
     mix_out[...] = (weighted[0] + weighted[1]).astype(kind).reshape(2, length, part_width)
-    swaps_mix = [swap(3, i, mix_out.at[i], mix_in, keep(mix_out, i, mix_in)) for i in BOTH]
+    swaps_mix = [swap(3, i, mix_out.at[i], mix_in, stay(mix_out, i, mix_in)) for i in BOTH]
     for start, _, _ in swaps_mix:
         start()
     for _, arrive, _ in swaps_hid + swaps_mix:
@@ -599,15 +689,18 @@
     @pl.loop(1, CTX)
     def _(k):
         stat_copy(k, ctx).wait_send()
-
-
-def project_and_mix(normed, residual, out_weight, router, ids, gate_w, up_w, down_w):
-    length, inner = normed.shape
+        state_copy(k, ctx).wait_send()
+        prior_copy(k, ctx).wait_send()
+
+
+def layer(query, key, value, decay, residual, out_weight, router, ids, gate_w, up_w, down_w):
+    length, inner = query.shape
+    head = inner // decay.shape[0]
     width = out_weight.shape[1]
     units, model = down_w.shape
     slots = CTX * (2 * length // EXP + length // 32)
     half_rows = slots // 2
-    kind, f32 = normed.dtype, jnp.float32
+    kind, f32 = query.dtype, jnp.float32
     vmem = pl.BlockSpec(memory_space=pltpu.VMEM)
     anywhere = pl.BlockSpec(memory_space=pl.ANY)
     two = (2, length, width)
@@ -617,9 +710,14 @@
     return pl.pallas_call(
         layer_kernel,
         out_shape=(out, out),
-        in_specs=[vmem] * 5 + [anywhere] * 3,
+        in_specs=[vmem] * 8 + [anywhere] * 3,
         out_specs=(vmem, vmem),
         scratch_shapes=[
+            pltpu.VMEM((CTX, head // 2 + 16, head), kind),
+            pltpu.VMEM((CTX, head // 2 + 16, head), kind),
+            pltpu.VMEM((CTX, head // 2, head), kind),
+            pltpu.VMEM((CTX, head // 2, head), kind),
+            pltpu.VMEM((length, inner), f32),
             pltpu.VMEM((CTX, length, inner), kind),
             pltpu.VMEM((4, 2 * length, width), kind),
             pltpu.VMEM((4, 2 * length, width), kind),
@@ -657,7 +755,7 @@
             pltpu.VMEM((2, 5, 2, half_rows, width), kind),
             pltpu.VMEM((EXP, PAD, width), kind),
             pltpu.VMEM((EXP, PAD, width), kind),
-            dma((3,)), dma((40,)), dma((40,)), dma((40,)), dma((40,)), dma((40,)), dma((40,)),
+            dma((3,)), dma((CTX,)), dma((CTX,)), dma((CTX,)), dma((CTX,)), dma((40,)), dma((40,)), dma((40,)), dma((40,)), dma((40,)), dma((40,)),
             dma((4,)), dma((4,)), dma((4,)), dma((4,)), dma((8,)), dma((8,)),
             dma((EXP,)), dma((EXP,)), dma((CTX,)), dma((CTX,)),
             dma((EXP,)), dma((EXP,)), dma((EXP,)), dma((EXP,)),
@@ -668,30 +766,7 @@
         cost_estimate=pl.CostEstimate(
             flops=6 * slots * model * units, bytes_accessed=6 * model * units, transcendentals=0
         ),
-    )(normed, residual, out_weight, router, ids, gate_w, up_w, down_w)
-
-
-def carried_in(array, axis, combine, identity):
-    size, index = (lax.axis_size(axis), lax.axis_index(axis))
-    everything = jax.tree.map(
-        lambda part, kind: lax.all_gather(part.astype(kind), axis),
-        array,
-        (jnp.bfloat16, jnp.bfloat16),
-    )
-    start = jax.tree.map(
-        lambda part, zero: jnp.broadcast_to(jnp.asarray(zero, part.dtype), part.shape),
-        array,
-        identity,
-    )
-
-    def step(k, before):
-        reached = k < index
-        new = combine(
-            before, jax.tree.map(lambda part, own: part[k].astype(own.dtype), everything, array)
-        )
-        return jax.tree.map(lambda a, b: jnp.where(reached, a, b), new, before)
-
-    return lax.fori_loop(0, size, step, start)
+    )(query, key, value, decay, residual, out_weight, router, ids, gate_w, up_w, down_w)
 
 
 def per_device(
@@ -707,47 +782,11 @@
     expert_up,
     expert_down,
 ):
-    length = query_rows.shape[0]
-    head_count = log_decay.shape[0]
-    head_width = query_rows.shape[1] // head_count
-    query_heads = query_rows.reshape(length, head_count, head_width)
-    key_heads = key_rows.reshape(length, head_count, head_width)
-    value_heads = value_rows.reshape(length, head_count, head_width)
-    cumulative = jnp.cumsum(log_decay, axis=1)
-    row_index = lax.broadcasted_iota(jnp.int32, (length, length), 0)
-    col_index = lax.broadcasted_iota(jnp.int32, (length, length), 1)
-    gaps = cumulative[:, :, None] - cumulative[:, None, :]
-    mask_weights = jnp.where((col_index <= row_index)[None], jnp.exp(jnp.minimum(gaps, 0.0)), 0.0)
-    scores = jnp.einsum("thd,shd->hts", query_heads, key_heads, preferred_element_type=jnp.float32)
-    scaled_scores = (scores * mask_weights).astype(jnp.bfloat16)
-    inside = jnp.einsum(
-        "hts,shd->thd", scaled_scores, value_heads, preferred_element_type=jnp.float32
-    )
-    block_total = cumulative[:, -1]
-    keep_factor = jnp.exp(block_total[:, None] - cumulative)
-    weighted_keys = key_heads.astype(jnp.float32) * keep_factor.T[:, :, None]
-    block_state = jnp.einsum(
-        "thd,the->hde", weighted_keys, value_heads.astype(jnp.float32), precision=highest
-    )
-
-    def combine_pair(earlier_pair, later_pair):
-        merged_total = earlier_pair[0] + later_pair[0]
-        merged_state = jnp.exp(later_pair[0])[:, None, None] * earlier_pair[1] + later_pair[1]
-        return (merged_total, merged_state)
-
-    empty_pair = (jnp.zeros_like(block_total), jnp.zeros_like(block_state))
-    prior_total, prior_state = carried_in(
-        (block_total, block_state), "ctx", combine_pair, empty_pair
-    )
-    outside = jnp.einsum(
-        "thd,hde->the", query_heads.astype(jnp.float32), prior_state, precision=highest
-    )
-    outside = outside * jnp.exp(cumulative).T[:, :, None]
-    attended = inside + outside
-    normed = attended * lax.rsqrt(jnp.mean(attended * attended, axis=2, keepdims=True) + epsilon)
-    normed = normed.astype(jnp.bfloat16).reshape(length, head_count * head_width)
-    return project_and_mix(
-        normed,
+    return layer(
+        query_rows,
+        key_rows,
+        value_rows,
+        log_decay,
         residual,
         out_weight,
         router_weight.T,

time: 277 us -> 201 us (0.73)
  blocking collectives: 30.4 us -> 0 us
  waiting for transfers between devices: 20.8 us -> 0 us
  other arithmetic: 18.8 us -> 0 us
  Pallas kernels: 180 us -> 197 us
  between operations: 14.8 us -> 0.64 us
  local copies, waits for them, and re-layouts: 7.16 us -> 3.23 us
    unnamed x1 -> x0, blocking collectives: 30.4 us -> none
    all_gather x1 -> x0, waiting for transfers between devices: 20.8 us -> none  [carried_in(): lax.all_gather(part.astype(kind), axis)]
    select_n x16 -> x0, other arithmetic: 17.5 us -> none  [step(): return jax.tree.map(lambda a, b: jnp.where(reached, a, b), new, before)]
    pallas_call x1, Pallas kernels: 180 us -> 197 us  [layer(): pl.pallas_call(layer_kernel, out_shape=(out, out), in_specs=[vmem] * 8 +...]
  transfers between devices with their start and end apart: 1 -> 0, of which waited for: 1 -> 0; matrix products, arithmetic and copies ran while one was open for 1% -> 0% of each run, Pallas kernels for 0% -> 0%
where the time goes in v3:
time: 201 us
  Pallas kernels  197 us (98%)
  local copies, waits for them, and re-layouts  3.23 us (2%)
    pallas_call x1, Pallas kernels, layer(): pl.pallas_call(layer_kernel, out_shape=(out, out), in_specs=[vmem] * 8 +...  197 us

profile of v3, /device:TPU:37, one launch (start us, length us, event | category | flops | bytes accessed | tf_op | source)
XLA Modules:
  0.0 201.2 jit_solution(6489530817888912103)
XLA Ops:
  0.6 197.3 %shard_map.122 = (bf16[128,768]{1,0:T(8,128)(2,1)}, bf16[128,768]{1,0:T(8,128)(2,1)}) custom-call(bf16[128,1024]{1,0:T(8,128)(2,1)} %query_ref.1, bf16[128,1024]{1,0:T(8,128)(2,1)} %key_ref.1, bf16[128,1024]{1,0:T(8,128)(2,1)} %value_ref.1, f32[8,128]{1,0:T(8,128)} %decay_ref.1, bf16[128,768]{1,0:T(8,128)(2,1)} %residual_ref.1, bf16[1024,384]{1,0:T(8,128)(2,1)} %out_w.1, ...), custom_call_target="tpu_custom_call" | custom-call | flops 12230590464 | bytes 21233664 | tf_op jit(solution)/shard_map/pallas_call | solution.py:710
  197.9 1.6 copy.15
  199.6 1.6 copy.16

commit v4 on v3

--- a/solution.py
+++ b/solution.py
@@ -10,6 +10,7 @@
 CTX = 16
 EXP = 8
 PAD = 80
+BACK = 48
 GROUPS = (0, -1, 1, 2)
 FAR_FIRST = (2, 1, -1, 0)
 BOTH = (0, 1)
@@ -74,40 +75,22 @@
     def arrive(self, half, ring, kind):
         self.copy(half, ring, kind, -1 if kind % 2 == 0 else 1).wait_recv()
 
-    def begin(self):
+    def blocks(self, ring):
         for half in BOTH:
-            self.send(half, 0, 0)
-            self.send(half, 0, 1)
+            self.send(half, ring, 0)
+            self.send(half, ring, 1)
+
+    def relay(self, ring):
         for half in BOTH:
-            self.send(half, 1, 0)
-            self.send(half, 1, 1)
-
-    def first_axis(self):
+            self.arrive(half, ring, 0)
+            self.send(half, ring, 2)
+            self.arrive(half, ring, 1)
+            self.send(half, ring, 3)
+
+    def settle(self, ring):
         for half in BOTH:
-            self.arrive(half, 0, 0)
-            self.send(half, 0, 2)
-            self.arrive(half, 0, 1)
-            self.send(half, 0, 3)
-        for ring in (2, 3):
-            for half in BOTH:
-                self.send(half, ring, 0)
-                self.send(half, ring, 1)
-        for half in BOTH:
-            self.arrive(half, 0, 2)
-            self.arrive(half, 0, 3)
-            self.send(half, 4, 0)
-            self.send(half, 4, 1)
-
-    def relay(self, group):
-        for half in BOTH:
-            self.arrive(half, group + 1, 0)
-            self.send(half, group + 1, 2)
-            self.arrive(half, group + 1, 1)
-            self.send(half, group + 1, 3)
-
-    def settle(self, half, group):
-        self.arrive(half, group + 1, 2)
-        self.arrive(half, group + 1, 3)
+            self.arrive(half, ring, 2)
+            self.arrive(half, ring, 3)
 
     def drain(self):
         for half in BOTH:
@@ -120,13 +103,10 @@
     def __init__(self, rel_out, rel_in, full_out, full_in, send_sem, recv_sem, base, device):
         self.refs = (rel_out, rel_in, full_out, full_in)
         self.send_sem, self.recv_sem, self.base, self.device = send_sem, recv_sem, base, device
-        self.sub = rel_out.shape[0] // 2
-
     def copy(self, kind):
         rel_out, rel_in, full_out, full_in = self.refs
         if kind < 2:
-            part = pl.ds(kind * self.sub, self.sub)
-            src, dst = rel_out.at[part], rel_in.at[part]
+            src, dst = rel_out.at[kind], rel_in.at[kind]
         else:
             src, dst = full_out.at[kind - 2], full_in.at[kind - 2]
         return pltpu.make_async_remote_copy(
@@ -147,12 +127,8 @@
     def near(self, way, value):
         _, rel_in, full_out, _ = self.refs
         full_out[way] = value.astype(full_out.dtype)
-        start = way * self.sub
-        part = pl.ds(start, self.sub)
         self.copy(way).wait_recv()
-        full_out[way, part] = (
-            value[start : start + self.sub] + rel_in[part].astype(jnp.float32)
-        ).astype(full_out.dtype)
+        full_out[way, way] = (value[way] + rel_in[way].astype(jnp.float32)).astype(full_out.dtype)
         self.copy(2 + way).start()
 
     def total(self, value):
@@ -172,9 +148,9 @@
     residual_ref, out_w, router_ref, ids_ref, gate_hbm, up_hbm, down_hbm,
     hidden_ref, mixture_ref,
     fresh_out, fresh_in, prior_out, prior_in, inside, normed_all, pair_out, pair_in, proj_rel_out, proj_rel_in, proj_full_out, proj_full_in,
-    res_out, res_in, ids_out, ids_in, hid_out, hid_in, mix_out, mix_in,
-    picks, disp_out, disp_in, stat_out, stat_in, scale_out, scale_in, scale_col, token_weight,
-    rows, gate_w, up_w, down_w, gate_acc, up_acc, active,
+    res_out, res_in, ids_out, ids_in, hid_out, hid_in, share_out, share_in,
+    picks, disp_out, disp_in, stat_out, stat_in, scale_out, scale_in, scale_col,
+    takes, rows, hidden_w, down_w, hidden_acc, active,
     rel_out, rel_in, full_out, full_in, ret_out, ret_in,
     weight_sem, f_send, f_recv, o_send, o_recv, n_send, n_recv, g_send, g_recv, r_send, r_recv, p_send, p_recv, q_send, q_recv,
     swap_send, swap_recv, d_send, d_recv, s_send, s_recv, c_send, c_recv, b_send, b_recv,
@@ -189,11 +165,18 @@
     half_rows = slots // 2
     model = down_w.shape[1]
     f32, kind = jnp.float32, rows.dtype
+    units = down_w.shape[0]
     place = ((y, z), (z, y))
 
     weight_copies = [
         pltpu.make_async_copy(src, dst, weight_sem.at[i])
-        for i, (src, dst) in enumerate(((gate_hbm, gate_w), (up_hbm, up_w), (down_hbm, down_w)))
+        for i, (src, dst) in enumerate(
+            (
+                (gate_hbm, hidden_w.at[pl.ds(0, units)]),
+                (up_hbm, hidden_w.at[pl.ds(units, units)]),
+                (down_hbm, down_w),
+            )
+        )
     ]
     for copy in weight_copies:
         copy.start()
@@ -250,12 +233,27 @@
         for i in BOTH:
             fresh_out[2 * h + i, 0:part_rows] = state[i * part_rows : (i + 1) * part_rows]
             fresh_out[2 * h + i, part_rows : part_rows + 16] = factor
+    def back_origin(i, k):
+        return {"ctx": y * SIDE + 2 * core + i, "exp": k}
+
+    def back_from_me(i, k):
+        return jnp.logical_and(2 * core + i == z, k == exp)
+
+    for i in BOTH:
+
+        @pl.loop(0, EXP)
+        def _(k):
+            @pl.when(jnp.logical_not(back_from_me(i, k)))
+            def _():
+                pl.semaphore_signal(barrier, inc=1, device_id=back_origin(i, k), device_id_type=MESH)
+
     ids_out[0:2, :] = ids_ref[...]
     for i in BOTH:
         res_out[i] = residual_ref[:, i * part_width : (i + 1) * part_width]
-    gate_acc[...] = jnp.zeros_like(gate_acc)
-    up_acc[...] = jnp.zeros_like(up_acc)
-    pl.semaphore_wait(barrier, CTX + EXP - 2 + jnp.where(exp == ctx // 2, 1, 2))
+    pl.semaphore_wait(
+        barrier,
+        CTX + EXP - 2 + jnp.where(exp == ctx // 2, 1, 2) + jnp.where(z // 2 == core, 15, 16),
+    )
 
     def swap(index, i, src, dst, mine):
         def copy(arriving):
@@ -351,6 +349,26 @@
 
     prior_in[ctx] = prior_out[ctx]
     grown = jnp.exp(cum_col)
+    hidden_acc[...] = jnp.zeros_like(hidden_acc)
+
+    expert_row = lax.broadcasted_iota(jnp.int32, (EXP, length), 0)
+    later = (
+        lax.broadcasted_iota(jnp.int32, (length, length), 0)
+        < lax.broadcasted_iota(jnp.int32, (length, length), 1)
+    ).astype(jnp.bfloat16)
+
+    def slots_of(ids):
+        chosen = [expert_row == ids[k : k + 1, :] for k in BOTH]
+        count = chosen[0].astype(f32) + chosen[1].astype(f32)
+        return chosen, count, dot(count.astype(jnp.bfloat16), later)
+
+    chosen, _, before = slots_of(ids_ref[...])
+    first_back = before + (expert_row * BACK).astype(f32)
+    spot = [jnp.sum(jnp.where(pick, first_back, 0.0), axis=0, keepdims=True) for pick in chosen]
+    spot_col = jnp.where(expert_row == 0, spot[0], jnp.where(expert_row == 1, spot[1], 0.0)).T
+    back_row = lax.broadcasted_iota(jnp.int32, (length, EXP * BACK), 1).astype(f32)
+    for k in BOTH:
+        takes[k] = jnp.where(back_row == spot_col[:, k : k + 1], 1.0, 0.0).astype(kind)
 
     @pl.loop(1, CTX)
     def _(k):
@@ -364,33 +382,25 @@
         normed_all[ctx, :, lanes] = (attended * lax.rsqrt(square + epsilon)).astype(kind)
 
     gather = Gather(normed_all, n_send, n_recv)
-    gather.begin()
+    gather.blocks(0)
+    gather.blocks(1)
     swaps_res = [swap(0, i, res_out.at[i], res_in, stay(res_out, i, res_in)) for i in BOTH]
     swaps_ids = [swap(1, i, ids_out, ids_in, stay_ids(i)) for i in BOTH]
     for start, _, _ in swaps_res + swaps_ids:
         start()
-    gather.first_axis()
     gather.relay(0)
-    gather.relay(1)
-    for half in BOTH:
-        gather.settle(half, 0)
-    gather.relay(2)
-    for half in BOTH:
-        gather.settle(half, 1)
-    gather.relay(3)
+    gather.blocks(2)
+    gather.blocks(3)
+    gather.settle(0)
+    gather.blocks(4)
+    for ring in range(1, 5):
+        gather.relay(ring)
     for _, arrive, _ in swaps_ids:
         arrive()
 
-    expert_row = lax.broadcasted_iota(jnp.int32, (EXP, length), 0)
-    later = (
-        lax.broadcasted_iota(jnp.int32, (length, length), 0)
-        < lax.broadcasted_iota(jnp.int32, (length, length), 1)
-    ).astype(jnp.bfloat16)
     named = []
     for i in BOTH:
-        chosen = [expert_row == ids_in[i, k : k + 1, :] for k in BOTH]
-        count = chosen[0].astype(f32) + chosen[1].astype(f32)
-        before = dot(count.astype(jnp.bfloat16), later)
+        chosen, count, before = slots_of(ids_in[i])
         key = jnp.where(count > 0.5, before + float(i * (pair_slots // 2)), -1.0)
         named.append((key, chosen))
     key = jnp.concatenate([named[0][0], named[1][0]], axis=1)
@@ -398,13 +408,14 @@
     for e in range(EXP):
         picks[e] = jnp.where(slot_row == key[e : e + 1, :], 1.0, 0.0).astype(picks.dtype)
 
-    for group in (2, 3):
-        for half in BOTH:
-            gather.settle(half, group)
+    for ring in range(1, 5):
+        gather.settle(ring)
 
     def project(x_to, core_to):
         blocks = normed_all[pl.ds(2 * (x_to * 2 + core_to), 2)]
-        return dot(blocks.reshape(2 * length, blocks.shape[2]), out_w[...])
+        return dot(blocks.reshape(2 * length, blocks.shape[2]), out_w[...]).reshape(
+            2, length, width
+        )
 
     def pair_copy(i):
         return pltpu.make_async_remote_copy(
@@ -435,8 +446,8 @@
             value = proj_sum.total(value)
     for _, arrive, _ in swaps_res:
         arrive()
-    hid = (res_in[...].reshape(2 * length, part_width).astype(f32) + value).astype(kind)
-    hid_out[...] = hid.reshape(2, length, part_width)
+    hid_out[...] = (res_in[...].astype(f32) + value).astype(kind)
+    hid = hid_out[...].reshape(2 * length, width)
 
     def disp_copy(k, src_exp):
         return pltpu.make_async_remote_copy(
@@ -448,14 +459,38 @@
             device_id_type=MESH,
         )
 
-    @pl.loop(1, EXP)
-    def _(k):
+    for k in (4, 3, 5, 2, 6, 7, 1):
         to = (exp + k) % EXP
         disp_out[to] = dot(picks[to, pl.ds(0, PAD), :], hid).astype(kind)
         disp_copy(k, exp).start()
 
     disp_in[exp] = dot(picks[exp, pl.ds(0, PAD), :], hid).astype(kind)
 
+    @pl.loop(1, EXP)
+    def _(k):
+        disp_copy(k, (exp + EXP - k) % EXP).wait_recv()
+
+    rows[ctx] = (
+        disp_in[...].astype(f32)[:, :pair_slots, :].reshape(slots, width).astype(kind)
+    )
+
+    def multiply(group, halves=BOTH):
+        for half in halves:
+            u, v = place[half]
+            chunks = [chunk_at(half, u + GROUPS[group], i) for i in range(SIDE)]
+            part_rows = pl.ds(half * half_rows, half_rows)
+            left = [rows[chunk, part_rows, :] for chunk in chunks]
+            right = [
+                hidden_w[:, pl.ds(pl.multiple_of(chunk * width, width), width)] for chunk in chunks
+            ]
+            hidden_acc[half] += dot_rows(
+                jnp.concatenate(left, axis=1), jnp.concatenate(right, axis=1)
+            )
+
+    spread = Gather(rows, g_send, g_recv)
+    spread.blocks(0)
+    spread.blocks(1)
+
     swaps_hid = [swap(2, i, hid_out.at[i], hid_in, stay(hid_out, i, hid_in)) for i in BOTH]
     for start, _, _ in swaps_hid:
         start()
@@ -463,10 +498,8 @@
     wide = hid.astype(f32)
     columns = pl.ds(pl.multiple_of(ctx * width, width), width)
     stat_out[pl.ds(0, EXP), :] = dot_rows(router_ref[:, columns], hid)
-    stat_out[pl.ds(EXP, EXP), :] = lax.dot_general(
-        jnp.ones((EXP, width), f32), wide * wide, (((1,), (1,)), ((), ())),
-        preferred_element_type=f32, precision=highest,
-    )
+    square = jnp.sum(wide * wide, axis=1, keepdims=True)
+    stat_out[pl.ds(EXP, EXP), :] = jnp.broadcast_to(square, (2 * length, 128)).T[:EXP]
     stat_in[ctx] = stat_out[...]
 
     def stat_copy(k, src_ctx):
@@ -483,31 +516,18 @@
     def _(k):
         stat_copy(k, ctx).start()
 
-    @pl.loop(1, EXP)
-    def _(k):
-        disp_copy(k, (exp + EXP - k) % EXP).wait_recv()
-
-    rows[ctx] = (
-        disp_in[...].astype(f32)[:, :pair_slots, :].reshape(slots, width).astype(kind)
-    )
-
-    def multiply(half, group):
-        u, v = place[half]
-        part_rows = pl.ds(half * half_rows, half_rows)
-
-        @pl.loop(0, SIDE)
-        def _(i):
-            chunk = chunk_at(half, u + GROUPS[group], i)
-            part = rows[chunk, part_rows, :]
-            depth = pl.ds(pl.multiple_of(chunk * width, width), width)
-            gate_acc[half] += dot_rows(part, gate_w[:, depth])
-            up_acc[half] += dot_rows(part, up_w[:, depth])
-
-    spread = Gather(rows, g_send, g_recv)
-    spread.begin()
-    spread.first_axis()
     spread.relay(0)
-
+    spread.settle(0)
+    spread.blocks(2)
+    spread.relay(1)
+    spread.blocks(3)
+
+    weight_copies[0].wait()
+    weight_copies[1].wait()
+    spread.settle(1)
+    spread.relay(2)
+    multiply(0)
+    spread.blocks(4)
     @pl.loop(1, CTX)
     def _(k):
         stat_copy(k, (ctx + CTX - k) % CTX).wait_recv()
@@ -535,13 +555,15 @@
             device_id_type=MESH,
         )
 
+    slot_scale = dot_rows(thirds, picks[...].reshape(EXP * 128, 2 * length))
+    for e in range(EXP):
+        scale_out[e] = slot_scale[:, e * 128 : (e + 1) * 128]
+
     @pl.loop(1, EXP)
     def _(k):
-        to = (exp + k) % EXP
-        scale_out[to] = dot_rows(thirds, picks[to])
         scale_copy(k, exp).start()
 
-    scale_in[exp] = dot_rows(thirds, picks[exp])
+    scale_in[exp] = scale_out[exp]
 
     picked = []
     for k in BOTH:
@@ -549,21 +571,19 @@
         picked.append(jnp.sum(jnp.where(chosen, logits, 0.0), axis=0, keepdims=True))
     first_weight = 1.0 / (1.0 + jnp.exp(picked[1] - picked[0]))
     second_weight = 1.0 / (1.0 + jnp.exp(picked[0] - picked[1]))
-    token_weight[...] = jnp.where(
-        which == 0, first_weight, jnp.where(which == 1, second_weight, 0.0)
-    ).T
-
-    weight_copies[0].wait()
-    weight_copies[1].wait()
-    spread.relay(1)
-    for half in BOTH:
-        spread.settle(half, 0)
-        multiply(half, 0)
-    spread.relay(2)
-    for half in BOTH:
-        spread.settle(half, 1)
-        multiply(half, 1)
+    share = jnp.where(which == 0, first_weight, jnp.where(which == 1, second_weight, 0.0))
+    for i in BOTH:
+        share_out[i] = share[:, i * length : (i + 1) * length]
+    swaps_share = [swap(3, i, share_out.at[i], share_in, stay(share_out, i, share_in)) for i in BOTH]
+    for start, _, _ in swaps_share:
+        start()
+
+    spread.settle(2)
     spread.relay(3)
+    multiply(1)
+    spread.settle(3)
+    spread.relay(4)
+    multiply(2)
 
     @pl.loop(1, EXP)
     def _(k):
@@ -574,22 +594,21 @@
         scale_col[pl.ds(e * pair_slots, pair_slots), :] = jnp.broadcast_to(
             row_scales[:pair_slots, e : e + 1], (pair_slots, 128)
         )
-    for half in BOTH:
-        spread.settle(half, 2)
-        multiply(half, 2)
-    for half in BOTH:
-        spread.settle(half, 3)
-        multiply(half, 3)
-        scale = scale_col[pl.ds(half * half_rows, half_rows), 0:1]
-        gate = gate_acc[half] * scale
-        up = up_acc[half] * scale
-        active[half] = (gate * (1.0 / (1.0 + jnp.exp(-gate))) * up).astype(kind)
     weight_copies[2].wait()
+    spread.settle(4)
+
+    row_blocks = slots // SIDE
 
     def product(half, du, dv):
         u, v = place[half]
-        chunk = chunk_at(half, u + dv, v + du)
-        return dot(active[half], down_w[:, pl.ds(pl.multiple_of(chunk * width, width), width)])
+        to = chunk_at(half, u + dv, v + du)
+        to_y, to_z = to // SIDE, to % SIDE
+        left = active[pl.ds(pl.multiple_of(to_y * row_blocks, 16), row_blocks), :]
+        out = []
+        for i in BOTH:
+            start = pl.multiple_of(((half * 2 + i) * SIDE + to_z) * width, width)
+            out.append(dot(left, down_w[:, pl.ds(start, width)]))
+        return jnp.stack(out)
 
     def ring_device(half, axis):
         return lambda step: {"ctx": plane_device(half, axis, step)}
@@ -606,24 +625,51 @@
         for half in BOTH
     ]
 
-    def back_copy(k, src_exp):
-        return pltpu.make_async_remote_copy(
-            src_ref=ret_out.at[(exp + k) % EXP],
-            dst_ref=ret_in.at[src_exp],
-            send_sem=b_send.at[k],
-            recv_sem=b_recv.at[k],
-            device_id={"exp": (exp + k) % EXP},
-            device_id_type=MESH,
-        )
-
-    for group in range(4):
-        for half in BOTH:
+    def back_copy(m):
+        to_exp = 2 * (m // SIDE) + z // 2
+        return pltpu.make_async_remote_copy(
+            src_ref=ret_out.at[m],
+            dst_ref=ret_in.at[z % 2, exp],
+            send_sem=b_send.at[m],
+            recv_sem=b_recv.at[(z % 2) * EXP + exp],
+            device_id={"ctx": y * SIDE + m % SIDE, "exp": to_exp},
+            device_id_type=MESH,
+        )
+
+    def back_arrival(i, k):
+        return pltpu.make_async_remote_copy(
+            src_ref=ret_out.at[0],
+            dst_ref=ret_in.at[i, k],
+            send_sem=b_send.at[0],
+            recv_sem=b_recv.at[i * EXP + k],
+            device_id=back_origin(i, k),
+            device_id_type=MESH,
+        )
+
+    def back_is_mine(m):
+        return jnp.logical_and(m % SIDE == z, 2 * (m // SIDE) + z // 2 == exp)
+
+    for half in BOTH:
+        multiply(3, (half,))
+        scale = scale_col[pl.ds(half * half_rows, half_rows), 0:1]
+        gate = hidden_acc[half, :, :units] * scale
+        up = hidden_acc[half, :, units:] * scale
+        active[pl.ds(half * half_rows, half_rows), :] = (
+            gate * (1.0 / (1.0 + jnp.exp(-gate))) * up
+        ).astype(kind)
+    for half in BOTH:
+        for group in range(4):
             sums[half][group].far(product(half, 2, FAR_FIRST[group]))
     for group in range(4):
         for half in BOTH:
             sums[half][group].near(0, product(half, 1, FAR_FIRST[group]))
             sums[half][group].near(1, product(half, -1, FAR_FIRST[group]))
-    blank = jnp.zeros((PAD - pair_slots, width), f32)
+    for _, arrive, _ in swaps_hid:
+        arrive()
+    for i in BOTH:
+        hidden_ref[:, i * part_width : (i + 1) * part_width] = hid_in[i]
+    block_slots = pair_slots // 2
+    blank = jnp.zeros((BACK - block_slots, width), f32)
     for group in range(4):
         for half in BOTH:
             value = sums[half][group].total(product(half, 0, FAR_FIRST[group]))
@@ -633,41 +679,19 @@
                 sums[half][4].near(group - 1, value)
             else:
                 value = sums[half][4].total(value)
-                for i in range(EXP // 2):
-                    part = value[i * pair_slots : (i + 1) * pair_slots]
-                    ret_out[half * (EXP // 2) + i] = jnp.concatenate([part, blank], axis=0).astype(kind)
-
-    @pl.loop(1, EXP)
-    def _(k):
-        back_copy(k, exp).start()
-
-    ret_in[exp] = ret_out[exp]
-
-    @pl.loop(1, EXP)
-    def _(k):
-        back_copy(k, (exp + EXP - k) % EXP).wait_recv()
-
-    back = ret_in[...].reshape(EXP * PAD, width)
-    weighted = []
-    for k in BOTH:
-        chosen = jnp.concatenate([named[0][1][k], named[1][1][k]], axis=1)
-        take = jnp.concatenate(
-            [
-                jnp.where(chosen[e : e + 1, :], picks[e, pl.ds(0, PAD), :].astype(f32), 0.0)
-                for e in range(EXP)
-            ],
-            axis=0,
-        ).T.astype(kind)
-        weighted.append((dot(take, back) * token_weight[:, k : k + 1]).astype(kind).astype(f32))
-    mix_out[...] = (weighted[0] + weighted[1]).astype(kind).reshape(2, length, part_width)
-    swaps_mix = [swap(3, i, mix_out.at[i], mix_in, stay(mix_out, i, mix_in)) for i in BOTH]
-    for start, _, _ in swaps_mix:
-        start()
-    for _, arrive, _ in swaps_hid + swaps_mix:
-        arrive()
-    for i in BOTH:
-        hidden_ref[:, i * part_width : (i + 1) * part_width] = hid_in[i]
-        mixture_ref[:, i * part_width : (i + 1) * part_width] = mix_in[i]
+                for m in range(half * EXP, half * EXP + EXP):
+                    start = m % SIDE * block_slots
+                    part = value[m // SIDE - 2 * half, start : start + block_slots]
+                    ret_out[m] = jnp.concatenate([part, blank], axis=0).astype(kind)
+                for m in range(half * EXP, half * EXP + EXP):
+
+                    @pl.when(back_is_mine(m))
+                    def _():
+                        ret_in[z % 2, exp] = ret_out[m]
+
+                    @pl.when(jnp.logical_not(back_is_mine(m)))
+                    def _():
+                        back_copy(m).start()
 
     gather.drain()
     spread.drain()
@@ -677,20 +701,44 @@
     for half in BOTH:
         for group in range(5):
             sums[half][group].drain()
-    for _, _, drain in swaps_res + swaps_ids + swaps_hid + swaps_mix:
+    for _, arrive, _ in swaps_share:
+        arrive()
+    for _, _, drain in swaps_res + swaps_ids + swaps_hid + swaps_share:
         drain()
 
     @pl.loop(1, EXP)
     def _(k):
         disp_copy(k, exp).wait_send()
         scale_copy(k, exp).wait_send()
-        back_copy(k, exp).wait_send()
 
     @pl.loop(1, CTX)
     def _(k):
         stat_copy(k, ctx).wait_send()
         state_copy(k, ctx).wait_send()
         prior_copy(k, ctx).wait_send()
+
+    share_col = share_in[0].T
+    for i in BOTH:
+
+        @pl.loop(0, EXP)
+        def _(k):
+            @pl.when(jnp.logical_not(back_from_me(i, k)))
+            def _():
+                back_arrival(i, k).wait_recv()
+
+        back = ret_in[i].reshape(EXP * BACK, width)
+        weighted = [
+            (dot(takes[k], back) * share_col[:, k : k + 1]).astype(kind).astype(f32) for k in BOTH
+        ]
+        mixture_ref[:, i * part_width : (i + 1) * part_width] = (weighted[0] + weighted[1]).astype(
+            kind
+        )
+
+    @pl.loop(0, 2 * EXP)
+    def _(m):
+        @pl.when(jnp.logical_not(back_is_mine(m)))
+        def _():
+            back_copy(m).wait_send()
 
 
 def layer(query, key, value, decay, residual, out_weight, router, ids, gate_w, up_w, down_w):
@@ -706,7 +754,7 @@
     two = (2, length, width)
     dma = pltpu.SemaphoreType.DMA
     out = jax.ShapeDtypeStruct(residual.shape, kind)
-    blocks = (2, 5, half_rows, width)
+    blocks = (2, 5, 2, slots // SIDE, width)
     return pl.pallas_call(
         layer_kernel,
         out_shape=(out, out),
@@ -719,20 +767,20 @@
             pltpu.VMEM((CTX, head // 2, head), kind),
             pltpu.VMEM((length, inner), f32),
             pltpu.VMEM((CTX, length, inner), kind),
-            pltpu.VMEM((4, 2 * length, width), kind),
-            pltpu.VMEM((4, 2 * length, width), kind),
-            pltpu.VMEM((2 * length, width), kind),
-            pltpu.VMEM((2 * length, width), kind),
-            pltpu.VMEM((2, 2 * length, width), kind),
-            pltpu.VMEM((2, 2 * length, width), kind),
+            pltpu.VMEM((4,) + two, kind),
+            pltpu.VMEM((4,) + two, kind),
+            pltpu.VMEM(two, kind),
+            pltpu.VMEM(two, kind),
+            pltpu.VMEM((2,) + two, kind),
+            pltpu.VMEM((2,) + two, kind),
             pltpu.VMEM(two, kind),
             pltpu.VMEM(two, kind),
             pltpu.VMEM((8, length), jnp.int32),
             pltpu.VMEM((2, 8, length), jnp.int32),
             pltpu.VMEM(two, kind),
             pltpu.VMEM(two, kind),
-            pltpu.VMEM(two, kind),
-            pltpu.VMEM(two, kind),
+            pltpu.VMEM((2, EXP, length), f32),
+            pltpu.VMEM((2, EXP, length), f32),
             pltpu.VMEM((EXP, 128, 2 * length), kind),
             pltpu.VMEM((EXP, PAD, width), kind),
             pltpu.VMEM((EXP, PAD, width), kind),
@@ -741,24 +789,22 @@
             pltpu.VMEM((EXP, 8, 128), f32),
             pltpu.VMEM((EXP, 8, 128), f32),
             pltpu.VMEM((slots, 128), f32),
-            pltpu.VMEM((2 * length, 8), f32),
+            pltpu.VMEM((2, length, EXP * BACK), kind),
             pltpu.VMEM((CTX, slots, width), kind),
+            pltpu.VMEM((2 * units, model), kind),
             pltpu.VMEM((units, model), kind),
-            pltpu.VMEM((units, model), kind),
-            pltpu.VMEM((units, model), kind),
-            pltpu.VMEM((2, half_rows, units), f32),
-            pltpu.VMEM((2, half_rows, units), f32),
-            pltpu.VMEM((2, half_rows, units), kind),
+            pltpu.VMEM((2, half_rows, 2 * units), f32),
+            pltpu.VMEM((slots, units), kind),
             pltpu.VMEM(blocks, kind),
             pltpu.VMEM(blocks, kind),
-            pltpu.VMEM((2, 5, 2, half_rows, width), kind),
-            pltpu.VMEM((2, 5, 2, half_rows, width), kind),
-            pltpu.VMEM((EXP, PAD, width), kind),
-            pltpu.VMEM((EXP, PAD, width), kind),
+            pltpu.VMEM((2, 5, 2) + blocks[2:], kind),
+            pltpu.VMEM((2, 5, 2) + blocks[2:], kind),
+            pltpu.VMEM((2 * EXP, BACK, width), kind),
+            pltpu.VMEM((2, EXP, BACK, width), kind),
             dma((3,)), dma((CTX,)), dma((CTX,)), dma((CTX,)), dma((CTX,)), dma((40,)), dma((40,)), dma((40,)), dma((40,)), dma((40,)), dma((40,)),
             dma((4,)), dma((4,)), dma((4,)), dma((4,)), dma((8,)), dma((8,)),
             dma((EXP,)), dma((EXP,)), dma((CTX,)), dma((CTX,)),
-            dma((EXP,)), dma((EXP,)), dma((EXP,)), dma((EXP,)),
+            dma((EXP,)), dma((EXP,)), dma((2 * EXP,)), dma((2 * EXP,)),
         ],
         compiler_params=pltpu.CompilerParams(
             collective_id=1, has_side_effects=True, vmem_limit_bytes=62 * 1024 * 1024

time: 201 us -> 187 us (0.930); the launches traced: 201 us -> 185 us
  Pallas kernels: 197 us -> 181 us
    pallas_call x1, Pallas kernels: 197 us -> 181 us  [layer(): pl.pallas_call(layer_kernel, out_shape=(out, out), in_specs=[vmem] * 8 +...]
where the time goes in v4:
time: 187 us; the launch traced here: 185 us
  Pallas kernels  181 us (97%)
  local copies, waits for them, and re-layouts  3.23 us (2%)
    pallas_call x1, Pallas kernels, layer(): pl.pallas_call(layer_kernel, out_shape=(out, out), in_specs=[vmem] * 8 +...  181 us

profile of v4, /device:TPU:37, one launch (start us, length us, event | category | flops | bytes accessed | tf_op | source)
XLA Modules:
  0.0 185.0 jit_solution(6903020766051956021)
XLA Ops:
  0.6 181.2 %shard_map.122 = (bf16[128,768]{1,0:T(8,128)(2,1)}, bf16[128,768]{1,0:T(8,128)(2,1)}) custom-call(bf16[128,1024]{1,0:T(8,128)(2,1)} %query_ref.1, bf16[128,1024]{1,0:T(8,128)(2,1)} %key_ref.1, bf16[128,1024]{1,0:T(8,128)(2,1)} %value_ref.1, f32[8,128]{1,0:T(8,128)} %decay_ref.1, bf16[128,768]{1,0:T(8,128)(2,1)} %residual_ref.1, bf16[1024,384]{1,0:T(8,128)(2,1)} %out_w.1, ...), custom_call_target="tpu_custom_call" | custom-call | flops 12230590464 | bytes 21233664 | tf_op jit(solution)/shard_map/pallas_call | solution.py:758
  181.8 1.6 copy.15
  183.4 1.6 copy.16

commit v5 on v4

--- a/solution.py
+++ b/solution.py
@@ -13,6 +13,10 @@
 BACK = 48
 GROUPS = (0, -1, 1, 2)
 FAR_FIRST = (2, 1, -1, 0)
+STEPS = sorted(
+    ((a, b) for a in range(4) for b in range(4) if a or b),
+    key=lambda step: -min(step[0], 4 - step[0]) - min(step[1], 4 - step[1]),
+)
 BOTH = (0, 1)
 epsilon = 1e-05
 highest = lax.Precision.HIGHEST
@@ -146,7 +150,7 @@
 def layer_kernel(
     query_ref, key_ref, value_ref, decay_ref,
     residual_ref, out_w, router_ref, ids_ref, gate_hbm, up_hbm, down_hbm,
-    hidden_ref, mixture_ref,
+    result_ref,
     fresh_out, fresh_in, prior_out, prior_in, inside, normed_all, pair_out, pair_in, proj_rel_out, proj_rel_in, proj_full_out, proj_full_in,
     res_out, res_in, ids_out, ids_in, hid_out, hid_in, share_out, share_in,
     picks, disp_out, disp_in, stat_out, stat_in, scale_out, scale_in, scale_col,
@@ -300,30 +304,36 @@
 
         return mine
 
-    def state_copy(k, src_ctx):
-        return pltpu.make_async_remote_copy(
-            src_ref=fresh_out.at[(ctx + k) % CTX],
+    def ctx_at(step, way):
+        return (y + way * step[0] + SIDE) % SIDE * SIDE + (z + way * step[1] + SIDE) % SIDE
+
+    def state_copy(step, src_ctx):
+        return pltpu.make_async_remote_copy(
+            src_ref=fresh_out.at[ctx_at(step, 1)],
             dst_ref=fresh_in.at[src_ctx],
-            send_sem=f_send.at[k],
-            recv_sem=f_recv.at[k],
-            device_id={"ctx": (ctx + k) % CTX},
-            device_id_type=MESH,
-        )
-
-    def prior_copy(k, src_ctx):
-        return pltpu.make_async_remote_copy(
-            src_ref=prior_out.at[(ctx + k) % CTX],
+            send_sem=f_send.at[step[0] * SIDE + step[1]],
+            recv_sem=f_recv.at[step[0] * SIDE + step[1]],
+            device_id={"ctx": ctx_at(step, 1)},
+            device_id_type=MESH,
+        )
+
+    def prior_copy(step, src_ctx):
+        return pltpu.make_async_remote_copy(
+            src_ref=prior_out.at[ctx_at(step, 1)],
             dst_ref=prior_in.at[src_ctx],
-            send_sem=o_send.at[k],
-            recv_sem=o_recv.at[k],
-            device_id={"ctx": (ctx + k) % CTX},
-            device_id_type=MESH,
-        )
-
-    @pl.loop(1, CTX)
-    def _(k):
-        state_copy(k, ctx).start()
-
+            send_sem=o_send.at[step[0] * SIDE + step[1]],
+            recv_sem=o_recv.at[step[0] * SIDE + step[1]],
+            device_id={"ctx": ctx_at(step, 1)},
+            device_id_type=MESH,
+        )
+
+    for step in STEPS:
+        state_copy(step, ctx).start()
+
+    swaps_res = [swap(0, i, res_out.at[i], res_in, stay(res_out, i, res_in)) for i in BOTH]
+    swaps_ids = [swap(1, i, ids_out, ids_in, stay_ids(i)) for i in BOTH]
+    for start, _, _ in swaps_ids:
+        start()
     fresh_in[ctx] = fresh_out[ctx]
     for h in range(heads):
         lanes = slice(h * head, (h + 1) * head)
@@ -332,9 +342,8 @@
         decayed = jnp.where(col_index <= row_index, jnp.exp(jnp.minimum(gaps, 0.0)), 0.0)
         inside[:, lanes] = dot((scores * decayed).astype(kind), value_ref[:, lanes])
 
-    @pl.loop(1, CTX)
-    def _(k):
-        state_copy(k, (ctx + CTX - k) % CTX).wait_recv()
+    for step in STEPS:
+        state_copy(step, ctx_at(step, -1)).wait_recv()
 
     state = jnp.zeros((part_rows, head), f32)
     for j in range(CTX):
@@ -343,9 +352,8 @@
             factor = fresh_in[j, part_rows : part_rows + 16].astype(f32)
             state = (factor[0:1] + factor[1:2]) * state + fresh_in[j, 0:part_rows].astype(f32)
 
-    @pl.loop(1, CTX)
-    def _(k):
-        prior_copy(k, ctx).start()
+    for step in STEPS:
+        prior_copy(step, ctx).start()
 
     prior_in[ctx] = prior_out[ctx]
     grown = jnp.exp(cum_col)
@@ -370,9 +378,8 @@
     for k in BOTH:
         takes[k] = jnp.where(back_row == spot_col[:, k : k + 1], 1.0, 0.0).astype(kind)
 
-    @pl.loop(1, CTX)
-    def _(k):
-        prior_copy(k, (ctx + CTX - k) % CTX).wait_recv()
+    for step in STEPS:
+        prior_copy(step, ctx_at(step, -1)).wait_recv()
 
     for h in range(heads):
         lanes = slice(h * head, (h + 1) * head)
@@ -384,10 +391,6 @@
     gather = Gather(normed_all, n_send, n_recv)
     gather.blocks(0)
     gather.blocks(1)
-    swaps_res = [swap(0, i, res_out.at[i], res_in, stay(res_out, i, res_in)) for i in BOTH]
-    swaps_ids = [swap(1, i, ids_out, ids_in, stay_ids(i)) for i in BOTH]
-    for start, _, _ in swaps_res + swaps_ids:
-        start()
     gather.relay(0)
     gather.blocks(2)
     gather.blocks(3)
@@ -395,6 +398,8 @@
     gather.blocks(4)
     for ring in range(1, 5):
         gather.relay(ring)
+    for start, _, _ in swaps_res:
+        start()
     for _, arrive, _ in swaps_ids:
         arrive()
 
@@ -464,6 +469,9 @@
         disp_out[to] = dot(picks[to, pl.ds(0, PAD), :], hid).astype(kind)
         disp_copy(k, exp).start()
 
+    swaps_hid = [swap(2, i, hid_out.at[i], hid_in, stay(hid_out, i, hid_in)) for i in BOTH]
+    for start, _, _ in swaps_hid:
+        start()
     disp_in[exp] = dot(picks[exp, pl.ds(0, PAD), :], hid).astype(kind)
 
     @pl.loop(1, EXP)
@@ -490,10 +498,6 @@
     spread = Gather(rows, g_send, g_recv)
     spread.blocks(0)
     spread.blocks(1)
-
-    swaps_hid = [swap(2, i, hid_out.at[i], hid_in, stay(hid_out, i, hid_in)) for i in BOTH]
-    for start, _, _ in swaps_hid:
-        start()
 
     wide = hid.astype(f32)
     columns = pl.ds(pl.multiple_of(ctx * width, width), width)
@@ -667,7 +671,7 @@
     for _, arrive, _ in swaps_hid:
         arrive()
     for i in BOTH:
-        hidden_ref[:, i * part_width : (i + 1) * part_width] = hid_in[i]
+        result_ref[0, :, i * part_width : (i + 1) * part_width] = hid_in[i]
     block_slots = pair_slots // 2
     blank = jnp.zeros((BACK - block_slots, width), f32)
     for group in range(4):
@@ -714,8 +718,10 @@
     @pl.loop(1, CTX)
     def _(k):
         stat_copy(k, ctx).wait_send()
-        state_copy(k, ctx).wait_send()
-        prior_copy(k, ctx).wait_send()
+
+    for step in STEPS:
+        state_copy(step, ctx).wait_send()
+        prior_copy(step, ctx).wait_send()
 
     share_col = share_in[0].T
     for i in BOTH:
@@ -730,7 +736,7 @@
         weighted = [
             (dot(takes[k], back) * share_col[:, k : k + 1]).astype(kind).astype(f32) for k in BOTH
         ]
-        mixture_ref[:, i * part_width : (i + 1) * part_width] = (weighted[0] + weighted[1]).astype(
+        result_ref[1, :, i * part_width : (i + 1) * part_width] = (weighted[0] + weighted[1]).astype(
             kind
         )
 
@@ -755,11 +761,11 @@
     dma = pltpu.SemaphoreType.DMA
     out = jax.ShapeDtypeStruct(residual.shape, kind)
     blocks = (2, 5, 2, slots // SIDE, width)
-    return pl.pallas_call(
+    results = pl.pallas_call(
         layer_kernel,
-        out_shape=(out, out),
+        out_shape=jax.ShapeDtypeStruct((2,) + residual.shape, kind),
         in_specs=[vmem] * 8 + [anywhere] * 3,
-        out_specs=(vmem, vmem),
+        out_specs=vmem,
         scratch_shapes=[
             pltpu.VMEM((CTX, head // 2 + 16, head), kind),
             pltpu.VMEM((CTX, head // 2 + 16, head), kind),
@@ -814,6 +820,17 @@
         ),
     )(query, key, value, decay, residual, out_weight, router, ids, gate_w, up_w, down_w)
 
+    def part_results(results_ref, hidden_ref, mixture_ref):
+        hidden_ref[...] = results_ref[0]
+        mixture_ref[...] = results_ref[1]
+
+    return pl.pallas_call(
+        part_results,
+        out_shape=(out, out),
+        in_specs=[vmem],
+        out_specs=(vmem, vmem),
+    )(results)
+
 
 def per_device(
     query_rows,

time: 187 us -> 184 us (0.984)
  local copies, waits for them, and re-layouts: 3.23 us -> 0 us
    unnamed x2 -> x0, local copies, waits for them, and re-layouts: 3.23 us -> none
    pallas_call x1 -> x2, Pallas kernels: 181 us -> 182 us  [the longest x1 180 us: layer(): pl.pallas_call(layer_kernel, out_shape=jax.ShapeDtypeStruct((2,) + residu...]
where the time goes in v5:
time: 184 us; the launch traced here: 182 us
  Pallas kernels  182 us (99%)
    pallas_call x1, Pallas kernels, layer(): pl.pallas_call(layer_kernel, out_shape=jax.ShapeDtypeStruct((2,) + residu...  180 us

profile of v5, /device:TPU:37, one launch (start us, length us, event | category | flops | bytes accessed | tf_op | source)
XLA Modules:
  0.0 182.2 jit_solution(8905870869322460427)
XLA Ops:
  0.6 179.8 %shard_map.122.results_ref = bf16[2,128,768]{2,1,0:T(8,128)(2,1)} custom-call(bf16[128,1024]{1,0:T(8,128)(2,1)} %query_ref.1, bf16[128,1024]{1,0:T(8,128)(2,1)} %key_ref.1, bf16[128,1024]{1,0:T(8,128)(2,1)} %value_ref.1, f32[8,128]{1,0:T(8,128)} %decay_ref.1, bf16[128,768]{1,0:T(8,128)(2,1)} %residual_ref.1, bf16[1024,384]{1,0:T(8,128)(2,1)} %out_w.1, ...), custom_call_target="tpu_custom_call" | custom-call | flops 12230590464 | bytes 21233664 | tf_op jit(solution)/shard_map/pallas_call | solution.py:764
  180.5 1.8 shard_map.123
